TPU v7x, 32 devices: a whole 2x2x4 slice. The times are simulated.
32 devices in a mesh: gx: 4 (over z), gy: 4 (over y, x), sa: 2 (over core).
Axes of the slice: x: 2, y: 2, z: 4, core: 2. Of those that a mesh axis runs over, the one named last changes fastest.
Arguments:
- field: float32 [33, 16, 168, 256], P(None, 'gx', 'gy', 'sa'), as said below
- start: float32 [33, 16], replicated, may hold values from -1 to 1
Outputs:
- basis: float32 [33, 16], replicated
- gram_two: float32 [168, 168], P('gy', ('gx', 'sa'))
Inputs may be any that keep to these rules, and one draw needn't show every extreme that they name: `field`: every entry is finite; species differ in scale.
All inputs are finite; a program needn't handle non-finite values.
Results may differ from a plain program's by a relative error of at most 0.0003.
Values sent between devices are 32-bit elements; how exact they have to be, the bound alone decides.
No kernel may reach another device: no remote copies, remote signals or barrier semaphores. Data moves between devices by JAX's collectives and lax.ppermute only.
A program may use at most 128 MiB of HBM per device.

v0:
```python
import jax
import jax.numpy as jnp
from jax import lax
from jax.sharding import PartitionSpec as P

ITERS = 4


HIGH = lax.Precision.HIGHEST


def orth(block):
    inner = jnp.dot(block.T, block, precision=HIGH, preferred_element_type=jnp.float32)
    lower = jnp.linalg.cholesky(inner)
    return jax.scipy.linalg.solve_triangular(lower, block.T, lower=True).T


def leading(gram, start, rounds):
    basis = orth(orth(start))
    for step in range(rounds):
        basis = orth(orth(jnp.dot(gram, basis, precision=HIGH, preferred_element_type=jnp.float32)))
    return basis


def project(basis, data):
    return jnp.einsum("sr,sxyz->rxyz", basis, data, precision=HIGH)


def line_gram(left, right):
    return jnp.einsum("rxiz,rxjz->ij", left, right, precision=HIGH)


def on_device(field, start):
    species, cells_x, cells_y, cells_z = field.shape
    ranks = start.shape[1]
    total_x = cells_x * lax.axis_size("gx")
    total_y = cells_y * lax.axis_size("gy")
    total_z = cells_z * lax.axis_size("sa")
    flat = field.reshape(species, -1)
    partial_gram = jnp.dot(flat, flat.T, precision=HIGH, preferred_element_type=jnp.float32)
    species_gram = lax.psum(partial_gram, ("gx", "gy", "sa")) / (total_x * total_y * total_z)
    basis = leading(species_gram, start, ITERS)
    moved = lax.all_to_all(project(basis, field), "gy", split_axis=3, concat_axis=2, tiled=True)
    rows = lax.psum_scatter(line_gram(moved, moved), "gy", scatter_dimension=0, tiled=True)
    block = lax.psum_scatter(rows, ("gx", "sa"), scatter_dimension=1, tiled=True) / (
        ranks * total_x * total_z
    )
    return (basis, block)


def solution(mesh):
    in_specs = (P(None, "gx", "gy", "sa"), P())
    out_specs = (P(), P("gy", ("gx", "sa")))
    return jax.shard_map(
        on_device, mesh=mesh, in_specs=in_specs, out_specs=out_specs, check_vma=False
    )
```

profile of v0, /device:TPU:0, one launch (start us, length us, event | category | flops | bytes accessed | tf_op | source)
XLA Modules:
  0.0 211.5 jit_solution(3804584794490085626)
XLA Ops:
  0.6 0.7 copy-done
  1.5 1.5 cholesky.164
  3.7 0.6 fusion.20
  4.3 1.2 custom-call.14
  6.0 1.5 cholesky.175
  7.5 0.6 compare_reduce_fusion.8
  8.1 0.6 fusion.21
  8.8 1.2 custom-call.15
  10.2 6.2 %fusion.5 = f32[33,33]{1,0:T(8,128)S(1)} fusion(f32[33,4,42,128]{3,1,2,0:T(4,128)} %param.5), kind=kOutput, calls=%fused_computation.6 | convolution fusion | flops 281014272 | bytes 2842884 | tf_op jit(solution)/shard_map/dot_general | solution.py:40
  16.4 42.4 %psum.7 = f32[33,33]{1,0:T(8,128)S(1)} all-reduce(f32[33,33]{1,0:T(8,128)S(1)} %fusion.5), channel_id=1, replica_groups=mesh['gx'=4,'gy'=4,'sa'=2] {'gx','gy','sa'}, use_global_device_ids=true, to_apply=%region_0.0 | all-reduce | flops 1089 | bytes 8712 | tf_op jit(solution)/shard_map/psum | solution.py:41
  59.1 1.5 cholesky.186
  61.3 0.6 fusion.22
  62.0 1.2 custom-call.16
  63.6 1.5 cholesky.197
  65.8 0.6 fusion.23
  66.4 1.2 custom-call.17
  68.2 1.5 cholesky.208
  70.4 0.6 fusion.24
  71.0 1.2 custom-call.18
  72.7 1.5 cholesky.219
  74.8 0.6 fusion.25
  75.5 1.2 custom-call.19
  77.3 1.5 cholesky.230
  79.4 0.6 fusion.26
  80.1 1.2 custom-call.20
  81.8 1.5 cholesky.241
  83.9 0.6 fusion.27
  84.6 1.2 custom-call.21
  86.4 1.5 cholesky.252
  88.5 0.6 fusion.28
  89.2 1.2 custom-call.22
  90.8 1.5 cholesky.263
  92.3 0.6 compare_reduce_fusion
  93.0 0.6 fusion.29
  93.6 1.2 custom-call.23
  95.1 3.3 %fusion.1 = f32[16,4,42,128]{3,0,2,1:T(8,128)} fusion(f32[33,4,42,128]{3,1,2,0:T(4,128)S(1)} %copy-done.1, f32[16,33]{1,0:T(8,128)S(1)} %fusion.31), kind=kOutput, calls=%fused_computation.1 | convolution fusion | flops 136249344 | bytes 4216896 | tf_op jit(solution)/shard_map/sr,sxyz->rxyz/dot_general | solution.py:26
  98.4 5.5 %copy.64 = f32[16,4,42,128]{2,0,1,3:T(8,128)} copy(f32[16,4,42,128]{3,0,2,1:T(8,128)} %fusion.1) | data formatting | bytes 2752512 | tf_op jit(solution)/shard_map/sr,sxyz->rxyz/dot_general | solution.py:26
  103.9 6.0 %reshape.20 = f32[4,1,86016]{2,1,0:T(1,128)S(1)} reshape(f32[128,4,16,42]{3,2,1,0:T(8,128)} %bitcast.165) | data formatting | bytes 2752512
  110.0 20.4 %all_to_all.18 = f32[4,1,86016]{2,1,0:T(1,128)S(1)} all-to-all(f32[4,1,86016]{2,1,0:T(1,128)S(1)} %reshape.20), channel_id=1, replica_groups=mesh['gx'=4,'gy'=4,'sa'=2] {'gy'}, dimensions={0} | all-to-all | bytes 2752512 | tf_op jit(solution)/shard_map/all_to_all | solution.py:43
  130.9 4.7 %reduce.4 = f32[4,86016]{1,0:T(4,128)S(1)} reduce(f32[4,1,86016]{2,1,0:T(1,128)S(1)} %all_to_all.18, f32[]{:T(128)} %broadcast.38), dimensions={1}, to_apply=%all_to_all.13.reduce_sub_computation | reduce | bytes 2752516 | tf_op jit(solution)/shard_map/all_to_all | solution.py:43
  135.6 7.7 %reshape.21 = f32[128,4,16,42]{3,2,1,0:T(8,128)} reshape(f32[4,86016]{1,0:T(4,128)S(1)} %reduce.4) | data formatting | bytes 2752512
  143.3 6.9 %copy.82 = f32[16,4,42,4,32]{2,3,4,1,0:T(4,128)} copy(f32[16,4,42,4,32]{2,0,1,4,3:T(8,128)} %bitcast.166) | data formatting | bytes 2752512 | tf_op jit(solution)/shard_map/all_to_all | solution.py:43
  150.2 4.2 %all_to_all.16 = f32[16,4,168,32]{2,3,1,0:T(8,128)S(1)} reshape(f32[16,4,4,42,32]{3,2,4,1,0:T(4,128)} %bitcast.167) | data formatting | bytes 2752512 | tf_op jit(solution)/shard_map/all_to_all | solution.py:43
  154.4 3.6 %convolution_bitcast_fusion = f32[168,168]{1,0:T(8,128)S(1)} fusion(f32[16,4,168,32]{2,3,1,0:T(8,128)S(1)} %all_to_all.16), kind=kOutput, calls=%fused_computation.5 | convolution fusion | flops 693633024 | bytes 1489152 | tf_op jit(solution)/shard_map/rxiz,rxjz->ij/dot_general | solution.py:30
  158.0 20.8 %fusion = f32[48,168]{1,0:T(8,128)S(1)} fusion(f32[168,168]{1,0:T(8,128)S(1)} %convolution_bitcast_fusion), kind=kCustom, calls=%all-reduce-scatter | all-reduce-scatter fusion | flops 32257 | bytes 145664
  178.8 2.5 %collective-permute-start = (f32[18,168]{1,0:T(8,128)S(1)}, f32[18,168]{1,0:T(8,128)S(1)}, u32[]{:S(2)}, u32[]{:S(2)}) collective-permute-start(f32[18,168]{1,0:T(8,128)S(1)} %slice.8), channel_id=1, source_target_pairs={{0,2},{2,4},{4,6},{1,3},{3,5},{5,7},{8,10},{10,12},{12,14},{9,11},... | collective-permute-start | bytes 36296
  184.0 26.7 %all-reduce.1 = f32[42,168]{1,0:T(8,128)S(1)} all-reduce(f32[42,168]{1,0:T(8,128)S(1)} %constant_dynamic-slice_fusion), channel_id=3, replica_groups=mesh['gx'=4,'gy'=4,'sa'=2] {'gx','sa'}, use_global_device_ids=true, to_apply=%region_4.7.clone | all-reduce | flops 7056 | bytes 56448
  210.8 0.7 copy.67
  (79 shorter events, 12.3 us)
Async XLA Ops:
  0.6 0.7 copy-start
  1.3 93.7 %copy-start.1 = (f32[33,4,42,128]{3,1,2,0:T(4,128)S(1)}, f32[33,4,42,128]{3,1,2,0:T(4,128)}, u32[]{:S(2)}) copy-start(f32[33,4,42,128]{3,1,2,0:T(4,128)} %param.5) | copy-start | bytes 8515588
  95.1 8.9 %copy-start.2 = (f32[16,33]{1,0:T(8,128)}, f32[16,33]{1,0:T(8,128)S(1)}, u32[]{:S(2)}) copy-start(f32[16,33]{1,0:T(8,128)S(1)} %fusion.31) | copy-start | bytes 6340
  154.4 26.9 %copy-start.3 = (u32[32]{0:T(128)S(1)}, u32[32]{0:T(128)}, u32[]{:S(2)}) copy-start(u32[32]{0:T(128)} %constant.40) | copy-start | bytes 388
  154.4 28.1 %copy-start.4 = (u32[32]{0:T(128)S(1)}, u32[32]{0:T(128)}, u32[]{:S(2)}) copy-start(u32[32]{0:T(128)} %constant.44) | copy-start | bytes 388
  178.8 5.0 %collective-permute-start = (f32[18,168]{1,0:T(8,128)S(1)}, f32[18,168]{1,0:T(8,128)S(1)}, u32[]{:S(2)}, u32[]{:S(2)}) collective-permute-start(f32[18,168]{1,0:T(8,128)S(1)} %slice.8), channel_id=1, source_target_pairs={{0,2},{2,4},{4,6},{1,3},{3,5},{5,7},{8,10},{10,12},{12,14},{9,11},... | collective-permute-start | bytes 36296
where the time goes:
time: 212 us
  blocking collectives  110 us (52%)
  other arithmetic  45.1 us (21%)
  local copies, waits for them, and re-layouts  34.3 us (16%)
  matrix products  17.1 us (8%)
  starting transfers between devices  2.47 us (1%)
  between operations  2.22 us (1%)
    unnamed x2, blocking collectives  47.5 us
    psum x1, blocking collectives, on_device(): lax.psum(partial_gram, ('gx', 'gy', 'sa')) / (total_x * total_y * total_z)  42.4 us
    another operation x30, other arithmetic, orth(): lower = jnp.linalg.cholesky(inner)  21.5 us
    all_to_all x1, blocking collectives, on_device(): lax.all_to_all(project(basis, field), 'gy', split_axis=3, concat_axis=2,...  20.4 us
    another operation x20, other arithmetic, orth(): return jax.scipy.linalg.solve_triangular(lower, block.T, lower=True).T  18.8 us
    unnamed x18, local copies, waits for them, and re-layouts  16.5 us
    all_to_all x3, local copies, waits for them, and re-layouts, on_device(): lax.all_to_all(project(basis, field), 'gy', split_axis=3, concat_axis=2,...  11.6 us
    dot_general x1, matrix products, on_device(): jnp.dot(flat, flat.T, precision=HIGH, preferred_element_type=jnp.float32)  6.16 us
  transfers between devices with their start and end apart: 1, of which 0 were waited for; matrix products, arithmetic and copies ran while one was open for 1% of the time, Pallas kernels for 0%

commit v1 on v0

v1 whole, which is shorter than its diff:
```python
import functools
import math

import jax
import jax.numpy as jnp
from jax import lax
from jax.experimental import pallas as pl
from jax.experimental.pallas import tpu as pltpu
from jax.sharding import PartitionSpec as P

ITERS = 4
LANES = 128
ROWS = 8
HIGH = lax.Precision.HIGHEST
BY_LAST = (((1,), (1,)), ((), ()))
ALL = ("gx", "gy", "sa")


def up(value, step):
    return -(-value // step) * step


def split(value):
    high = value.astype(jnp.bfloat16)
    low = (value - high.astype(jnp.float32)).astype(jnp.bfloat16)
    return high, low


def dot32(left, right, dims):
    return lax.dot_general(left, right, dims, preferred_element_type=jnp.float32)


def triangle(species):
    places, at = [], 0
    for top in range(0, species, ROWS):
        places.append((top, at))
        at += species - top
    return places, at


def gram_kernel(field_ref, out_ref, total):
    step = pl.program_id(0)
    species, _, lines, cells = field_ref.shape
    flat = jnp.concatenate([field_ref[:, 0, y, :] for y in range(lines)], axis=1)
    part = lax.dot_general(flat, flat, BY_LAST, precision=HIGH, preferred_element_type=jnp.float32)

    @pl.when(step == 0)
    def _():
        total[...] = jnp.zeros_like(total)

    total[:species, :species] += part

    @pl.when(step == pl.num_programs(0) - 1)
    def _():
        lane = lax.broadcasted_iota(jnp.int32, (ROWS, LANES), 1)
        tile = jnp.zeros((ROWS, LANES), jnp.float32)
        for top, at in triangle(species)[0]:
            rows = pltpu.roll(total[top : top + ROWS, :], (at - top) % LANES, 1)
            tile = jnp.where((lane >= at) & (lane < at + species - top), rows, tile)
        out_ref[...] = jnp.broadcast_to(tile[None], out_ref.shape)


def gram_tiles(field, devices):
    species, cells_x, lines, cells = field.shape
    return pl.pallas_call(
        gram_kernel,
        grid=(cells_x,),
        in_specs=[pl.BlockSpec((species, 1, lines, cells), lambda i: (0, i, 0, 0))],
        out_specs=pl.BlockSpec((devices, ROWS, LANES), lambda i: (0, 0, 0)),
        out_shape=jax.ShapeDtypeStruct((devices, ROWS, LANES), jnp.float32),
        scratch_shapes=[pltpu.VMEM((up(species, ROWS), LANES), jnp.float32)],
        compiler_params=pltpu.CompilerParams(vmem_limit_bytes=40 * 2**20),
        name="gram_tiles",
    )(field)


def orth(rows):
    ranks = rows.shape[0]
    inner = lax.dot_general(rows, rows, BY_LAST, precision=HIGH, preferred_element_type=jnp.float32)
    columns = [jnp.broadcast_to(inner[:, k : k + 1], (ranks, LANES)) for k in range(ranks)]
    index = lax.broadcasted_iota(jnp.int32, (ranks, LANES), 0)
    pivots = jnp.ones((ranks, LANES), jnp.float32)
    for k in range(ranks):
        pivot = columns[k][k : k + 1, :]
        factor = jnp.where(index > k, columns[k] * (1.0 / pivot), 0.0)
        pivots = jnp.where(index == k, pivot, pivots)
        for j in range(k + 1, ranks):
            columns[j] = columns[j] - factor * columns[j][k : k + 1, :]
        rows = rows - factor * rows[k : k + 1, :]
    return rows * lax.rsqrt(pivots)


def start_kernel(start_ref, out_ref):
    out_ref[...] = orth(orth(start_ref[...]))


def basis_kernel(species, scale, tiles_ref, start_ref, rows_ref, basis_ref):
    tile = jnp.sum(tiles_ref[...], axis=0) * scale
    places, _ = triangle(species)
    parts = [pltpu.roll(tile, (top - at) % LANES, 1) for top, at in places]
    parts += [jnp.zeros((ROWS, LANES), jnp.float32)] * (LANES // ROWS - len(parts))
    upper = jnp.concatenate(parts, axis=0)
    row = lax.broadcasted_iota(jnp.int32, (LANES, LANES), 0)
    column = lax.broadcasted_iota(jnp.int32, (LANES, LANES), 1)
    gram = jnp.where(column >= row // ROWS * ROWS, upper, upper.T)
    gram = jnp.where((row < species) & (column < species), gram, 0.0)
    rows = start_ref[...]
    for _ in range(ITERS):
        rows = orth(orth(jnp.dot(rows, gram, precision=HIGH, preferred_element_type=jnp.float32)))
    rows_ref[...] = rows
    basis_ref[...] = rows.T[:species, :]


def whole_call(kernel, out_shape, name, *args):
    return pl.pallas_call(
        kernel,
        out_shape=out_shape,
        compiler_params=pltpu.CompilerParams(vmem_limit_bytes=40 * 2**20),
        name=name,
    )(*args)


def core_kernel(count, me_ref, rows_ref, field_ref, *out_refs):
    del me_ref
    step = pl.program_id(0)
    species, _, lines, cells = field_ref.shape
    ranks = rows_ref.shape[0]
    flat = jnp.concatenate([field_ref[:, 0, y, :] for y in range(lines)], axis=1)
    high, low = split(flat)
    basis_high, basis_low = split(rows_ref[:, :species])
    dims = (((1,), (0,)), ((), ()))
    both = dot32(jnp.concatenate([basis_high, basis_low], axis=0), high, dims)
    core = both[:ranks] + both[ranks:] + dot32(basis_high, low, dims)
    for k in range(count):

        @pl.when(step == k)
        def _(k=k):
            for y in range(lines):
                out_refs[k][y] = core[:, y * cells : (y + 1) * cells]


def core_pieces(rows, field, me, count):
    species, cells_x, lines, cells = field.shape
    ranks = rows.shape[0]
    piece = (lines, ranks, cells)
    return pl.pallas_call(
        functools.partial(core_kernel, count),
        grid_spec=pltpu.PrefetchScalarGridSpec(
            num_scalar_prefetch=1,
            grid=(count,),
            in_specs=[
                pl.BlockSpec(rows.shape, lambda i, me: (0, 0)),
                pl.BlockSpec((species, 1, lines, cells), lambda i, me: (0, me[i], 0, 0)),
            ],
            out_specs=[pl.BlockSpec(piece, lambda i, me: (0, 0, 0))] * count,
        ),
        out_shape=[jax.ShapeDtypeStruct(piece, jnp.float32)] * count,
        compiler_params=pltpu.CompilerParams(vmem_limit_bytes=40 * 2**20),
        name="core_pieces",
    )(me, rows, field)


def packing(lines, columns):
    groups = LANES // lines
    deep = -(-columns // groups)
    return groups, deep, up(deep, ROWS)


def line_kernel(axes, order_ref, *refs):
    n_gx, n_gy, n_sa = axes
    pieces, (out_ref, high_ref, low_ref, gram_ref) = refs[:n_gy], refs[n_gy:]
    lines, ranks, cells = pieces[0].shape
    pitch = high_ref.shape[0] // n_gy
    high_ref[...] = jnp.zeros_like(high_ref)
    low_ref[...] = jnp.zeros_like(low_ref)
    for k in range(n_gy):
        at = pl.multiple_of(order_ref[k] * pitch, pitch)
        for r in range(ranks):
            block = jnp.concatenate(
                [pieces[k][:, r, :], jnp.zeros((pitch - lines, cells), jnp.float32)], axis=0
            )
            high, low = split(block)
            high_ref[pl.ds(at, pitch), r * cells : (r + 1) * cells] = high
            low_ref[pl.ds(at, pitch), r * cells : (r + 1) * cells] = low
    size = n_gy * pitch
    gram_ref[...] = jnp.zeros_like(gram_ref)
    gram_ref[:size, :size] = dot32(high_ref[...], low_ref[...], BY_LAST)
    cross = gram_ref[:size, :size]
    gram_ref[:size, :size] = dot32(high_ref[...], high_ref[...], BY_LAST) + cross + cross.T
    wide = gram_ref.shape[1]
    columns = lines * n_gy // (n_gx * n_sa)
    groups, deep, tall = packing(lines, columns)
    lane = lax.broadcasted_iota(jnp.int32, (tall, LANES), 1)
    for c in range(n_gx * n_sa):
        first = c * columns
        base = first // lines * pitch + first % lines
        bands = [gram_ref[base + g * deep : base + g * deep + tall, :] for g in range(groups)]
        for i in range(n_gy):
            tile = jnp.zeros((tall, LANES), jnp.float32)
            for g in range(groups):
                moved = pltpu.roll(bands[g], (g * lines - i * pitch) % wide, 1)[:, :LANES]
                tile = jnp.where((lane >= g * lines) & (lane < (g + 1) * lines), moved, tile)
            out_ref[((c // n_sa) * n_gy + i) * n_sa + c % n_sa] = tile


def line_tiles(pieces, order, axes):
    n_gx, n_gy, n_sa = axes
    lines, ranks, cells = pieces[0].shape
    pitch = up(lines, 16)
    columns = lines * n_gy // (n_gx * n_sa)
    _, _, tall = packing(lines, columns)
    size = n_gy * pitch
    return pl.pallas_call(
        functools.partial(line_kernel, axes),
        in_specs=[pl.BlockSpec(memory_space=pltpu.SMEM)]
        + [pl.BlockSpec(memory_space=pltpu.VMEM)] * n_gy,
        out_specs=pl.BlockSpec(memory_space=pltpu.VMEM),
        out_shape=jax.ShapeDtypeStruct((n_gx * n_gy * n_sa, tall, LANES), jnp.float32),
        scratch_shapes=[
            pltpu.VMEM((size, ranks * cells), jnp.bfloat16),
            pltpu.VMEM((size, ranks * cells), jnp.bfloat16),
            pltpu.VMEM((size + tall, up(size, LANES)), jnp.float32),
        ],
        compiler_params=pltpu.CompilerParams(vmem_limit_bytes=40 * 2**20),
        name="line_tiles",
    )(order, *pieces)


def block_kernel(scale, tiles_ref, out_ref):
    lines, columns = out_ref.shape
    groups, deep, tall = packing(lines, columns)
    tile = jnp.sum(tiles_ref[...], axis=0) * scale
    parts = [tile if g == 0 else pltpu.roll(tile, LANES - g * lines, 1) for g in range(groups)]
    high = groups * tall
    stack = jnp.concatenate(parts + [jnp.zeros((LANES - high, LANES), jnp.float32)], axis=0).T
    lane = lax.broadcasted_iota(jnp.int32, (LANES, LANES), 1)
    out = stack
    for g in range(1, groups):
        moved = pltpu.roll(stack, LANES - g * (tall - deep), 1)
        out = jnp.where(lane >= g * deep, moved, out)
    out_ref[...] = out[:lines, :columns]


def exchange(piece, axis, size, k):
    if size & (size - 1):
        raise ValueError("axis size")
    return lax.ppermute(piece, axis, [(a, a ^ k) for a in range(size)])


def on_device(field, start):
    species, cells_x, lines, cells_z = field.shape
    ranks = start.shape[1]
    n_gx, n_gy, n_sa = lax.axis_size("gx"), lax.axis_size("gy"), lax.axis_size("sa")
    devices = n_gx * n_gy * n_sa
    total_x, total_y, total_z = cells_x * n_gx, lines * n_gy, cells_z * n_sa
    columns = total_y // (n_gx * n_sa)
    me = lax.axis_index("gy")
    order = jnp.bitwise_xor(jnp.arange(n_gy, dtype=jnp.int32), me.astype(jnp.int32))

    first = whole_call(
        start_kernel,
        jax.ShapeDtypeStruct((ranks, LANES), jnp.float32),
        "start_rows",
        jnp.pad(start.T, ((0, 0), (0, LANES - species))),
    )
    tiles = lax.all_to_all(gram_tiles(field, devices), ALL, 0, 0, tiled=True)
    rows, basis = whole_call(
        functools.partial(basis_kernel, species, 1.0 / (total_x * total_y * total_z)),
        [
            jax.ShapeDtypeStruct((ranks, LANES), jnp.float32),
            jax.ShapeDtypeStruct((species, ranks), jnp.float32),
        ],
        "basis_rows",
        tiles,
        first,
    )
    scale = 1.0 / (ranks * total_x * total_z)
    parts_x = math.gcd(n_gy, cells_x)
    parts_z = n_gy // parts_x
    if parts_x == cells_x and parts_z == 1:
        pieces = core_pieces(rows, field, order, n_gy)
        deep = cells_z
    else:
        wide_x, wide_z = cells_x // parts_x, cells_z // parts_z
        core = jnp.einsum("rs,sxyz->yrxz", rows[:, :species], field, precision=HIGH)
        pieces = []
        for k in range(n_gy):
            at = jnp.bitwise_xor(me, k)
            cut = lax.dynamic_slice(
                core,
                (0, 0, at // parts_z * wide_x, at % parts_z * wide_z),
                (lines, ranks, wide_x, wide_z),
            )
            pieces.append(cut.reshape(lines, -1, LANES))
    pieces = [pieces[0]] + [exchange(pieces[k], "gy", n_gy, k) for k in range(1, n_gy)]
    blocks = lax.all_to_all(line_tiles(pieces, order, (n_gx, n_gy, n_sa)), ALL, 0, 0, tiled=True)
    block = whole_call(
        functools.partial(block_kernel, scale),
        jax.ShapeDtypeStruct((lines, columns), jnp.float32),
        "own_block",
        blocks,
    )
    return (basis, block)


def solution(mesh):
    in_specs = (P(None, "gx", "gy", "sa"), P())
    out_specs = (P(), P("gy", ("gx", "sa")))
    return jax.shard_map(
        on_device, mesh=mesh, in_specs=in_specs, out_specs=out_specs, check_vma=False
    )
```

time: 212 us -> 63.3 us (0.30)
  blocking collectives: 110 us -> 0 us
  other arithmetic: 45.1 us -> 0.01 us
  local copies, waits for them, and re-layouts: 34.3 us -> 3.47 us
  waiting for transfers between devices: 0.01 us -> 29.1 us
  matrix products: 17.1 us -> 0 us
  Pallas kernels: 0 us -> 16.3 us
  starting transfers between devices: 2.47 us -> 13.4 us
    unnamed x2 -> x0, blocking collectives: 47.5 us -> none
    psum x1 -> x0, blocking collectives: 42.4 us -> none  [on_device(): lax.psum(partial_gram, ('gx', 'gy', 'sa')) / (total_x * total_y * total_z)]
    another operation x50 -> x0, other arithmetic: 40.2 us -> none  [the longest x30 21.5 us: orth(): lower = jnp.linalg.cholesky(inner)]
    all_to_all x1 -> x0, blocking collectives: 20.4 us -> none  [on_device(): lax.all_to_all(project(basis, field), 'gy', split_axis=3, concat_axis=2,...]
    pallas_call x0 -> x6, Pallas kernels: none -> 16.3 us  [the longest x3 5.25 us: whole_call(): pl.pallas_call(kernel, out_shape=out_shape, compiler_params=pltpu.Compile...]
    dot_general x17 -> x0, matrix products: 15.1 us -> none  [the longest x1 6.16 us: on_device(): jnp.dot(flat, flat.T, precision=HIGH, preferred_element_type=jnp.float32)]
    all_to_all x0 -> x2, waiting for transfers between devices: none -> 14.9 us  [the longest x1 7.55 us: on_device(): lax.all_to_all(line_tiles(pieces, order, (n_gx, n_gy, n_sa)), ALL, 0, 0,...]
    ppermute x0 -> x3, waiting for transfers between devices: none -> 14.1 us  [exchange(): return lax.ppermute(piece, axis, [(a, a ^ k) for a in range(size)])]
  transfers between devices with their start and end apart: 1 -> 5, of which waited for: 0 -> 4; matrix products, arithmetic and copies ran while one was open for 1% -> 1% of each run, Pallas kernels for 0% -> 1%
where the time goes in v1:
time: 63.3 us; the launch traced here: 63 us
  waiting for transfers between devices  29.1 us (46%)
  Pallas kernels  16.3 us (26%)
  starting transfers between devices  13.4 us (21%)
  local copies, waits for them, and re-layouts  3.47 us (5%)
  between operations  0.72 us (1%)
    ppermute x3, waiting for transfers between devices, exchange(): return lax.ppermute(piece, axis, [(a, a ^ k) for a in range(size)])  14.1 us
    all_to_all x1, waiting for transfers between devices, on_device(): lax.all_to_all(line_tiles(pieces, order, (n_gx, n_gy, n_sa)), ALL, 0, 0,...  7.55 us
    all_to_all x1, waiting for transfers between devices, on_device(): tiles = lax.all_to_all(gram_tiles(field, devices), ALL, 0, 0, tiled=True)  7.36 us
    all_to_all x1, starting transfers between devices, on_device(): tiles = lax.all_to_all(gram_tiles(field, devices), ALL, 0, 0, tiled=True)  7.29 us
    pallas_call x3, Pallas kernels, whole_call(): pl.pallas_call(kernel, out_shape=out_shape, compiler_params=pltpu.Compile...  5.25 us
    pallas_call x1, Pallas kernels, gram_tiles(): pl.pallas_call(gram_kernel, grid=(cells_x,), in_specs=[pl.BlockSpec((spec...  4.41 us
    ppermute x3, starting transfers between devices, exchange(): return lax.ppermute(piece, axis, [(a, a ^ k) for a in range(size)])  3.55 us
    pallas_call x1, Pallas kernels, core_pieces(): pl.pallas_call(functools.partial(core_kernel, count), grid_spec=pltpu.Pre...  3.51 us
  transfers between devices with their start and end apart: 5, of which 4 were waited for; matrix products, arithmetic and copies ran while one was open for 1% of the time, Pallas kernels for 1%

profile of v1, /device:TPU:0, one launch (start us, length us, event | category | flops | bytes accessed | tf_op | source)
XLA Modules:
  0.0 63.0 jit_solution(14881397064267058888)
XLA Ops:
  0.6 2.1 %copy.4.field_ref = f32[33,4,42,128]{3,2,1,0:T(8,128)S(1)} copy(f32[33,4,42,128]{3,1,2,0:T(4,128)} %param.2) | data formatting | bytes 5677056 | tf_op args[0]
  2.7 0.0 copy-start
  2.7 4.4 %gram_tiles.1 = f32[32,8,128]{2,1,0:T(8,128)} custom-call(f32[33,4,42,128]{3,2,1,0:T(8,128)S(1)} %copy.4.field_ref), custom_call_target="tpu_custom_call" | custom-call | tf_op jit(solution)/shard_map/gram_tiles/pallas_call | solution.py:65
  7.2 7.3 %all-to-all-start = ((f32[32,8,128]{2,1,0:T(8,128)}), f32[32,8,128]{2,1,0:T(8,128)S(1)}, u32[]{:S(2)}, u32[]{:S(2)}) async-start(f32[32,8,128]{2,1,0:T(8,128)} %gram_tiles.1), calls=%async_computation | async-start | bytes 262144 | tf_op jit(solution)/shard_map/all_to_all | solution.py:266
  14.5 0.0 copy-done
  14.5 0.8 %start_rows.1.start_ref = f32[16,128]{1,0:T(8,128)S(1)} custom-call(f32[16,128]{1,0:T(8,128)S(1)} %pad.4.start_ref), custom_call_target="tpu_custom_call" | custom-call | tf_op jit(solution)/shard_map/start_rows/pallas_call | solution.py:115
  15.3 7.4 %all-to-all-done.tiles_ref = f32[32,8,128]{2,1,0:T(8,128)S(1)} async-done(((f32[32,8,128]{2,1,0:T(8,128)}), f32[32,8,128]{2,1,0:T(8,128)S(1)}, u32[]{:S(2)}, u32[]{:S(2)}) %all-to-all-start) | async-done | bytes 131104 | tf_op jit(solution)/shard_map/all_to_all | solution.py:266
  22.7 4.2 %basis_rows.1 = (f32[16,128]{1,0:T(8,128)S(1)}, f32[33,16]{1,0:T(8,128)S(1)}) custom-call(f32[32,8,128]{2,1,0:T(8,128)S(1)} %all-to-all-done.tiles_ref, f32[16,128]{1,0:T(8,128)S(1)} %start_rows.1.start_ref), custom_call_target="tpu_custom_call" | custom-call | tf_op jit(solution)/shard_map/basis_rows/pallas_call | solution.py:115
  26.9 3.5 %core_pieces.1 = (f32[42,16,128]{2,1,0:T(8,128)S(1)}, f32[42,16,128]{2,1,0:T(8,128)S(1)}, f32[42,16,128]{2,1,0:T(8,128)S(1)}, f32[42,16,128]{2,1,0:T(8,128)S(1)}) custom-call(s32[4]{0:T(128)S(1)} %iota_xor_fusion.me_ref.order_ref, f32[16,128]{1,0:T(8,128)S(1)} %get-tuple-element.9.rows_ref, f32[33,4,42,128]{3,2,1,0:T(8,128)S(1)} %copy.4.field_ref), custom_call_target="tpu_custom_call" | custom-call | tf_op jit(solution)/shard_map/core_pieces/pallas_call | solution.py:146
  30.4 0.5 collective-permute-start
  30.9 1.0 %collective-permute-start.1 = (f32[42,16,128]{2,1,0:T(8,128)S(1)}, f32[42,16,128]{2,1,0:T(8,128)S(1)}, u32[]{:S(2)}, u32[]{:S(2)}) collective-permute-start(f32[42,16,128]{2,1,0:T(8,128)S(1)} %get-tuple-element.12), channel_id=1, source_target_pairs={{0,4},{2,6},{4,0},{6,2},{1,5},{3,7},{5,1},{7,3},{8,12},{10,14},{12... | collective-permute-start | bytes 1032200 | tf_op jit(solution)/shard_map/ppermute | solution.py:247
  31.9 2.1 %collective-permute-start.2 = (f32[42,16,128]{2,1,0:T(8,128)S(1)}, f32[42,16,128]{2,1,0:T(8,128)S(1)}, u32[]{:S(2)}, u32[]{:S(2)}) collective-permute-start(f32[42,16,128]{2,1,0:T(8,128)S(1)} %get-tuple-element.13), channel_id=1, source_target_pairs={{0,6},{2,4},{4,2},{6,0},{1,7},{3,5},{5,3},{7,1},{8,14},{10,12},{12... | collective-permute-start | bytes 1032200 | tf_op jit(solution)/shard_map/ppermute | solution.py:247
  33.9 7.4 %collective-permute-done.refs_1_ = f32[42,16,128]{2,1,0:T(8,128)S(1)} collective-permute-done((f32[42,16,128]{2,1,0:T(8,128)S(1)}, f32[42,16,128]{2,1,0:T(8,128)S(1)}, u32[]{:S(2)}, u32[]{:S(2)}) %collective-permute-start) | collective-permute-done | bytes 344096 | tf_op jit(solution)/shard_map/ppermute | solution.py:247
  41.3 6.7 %collective-permute-done.1.refs_2_ = f32[42,16,128]{2,1,0:T(8,128)S(1)} collective-permute-done((f32[42,16,128]{2,1,0:T(8,128)S(1)}, f32[42,16,128]{2,1,0:T(8,128)S(1)}, u32[]{:S(2)}, u32[]{:S(2)}) %collective-permute-start.1) | collective-permute-done | bytes 344096 | tf_op jit(solution)/shard_map/ppermute | solution.py:247
  48.1 0.0 collective-permute-done.2.refs_3_
  48.1 3.2 %line_tiles.1 = f32[32,8,128]{2,1,0:T(8,128)} custom-call(s32[4]{0:T(128)S(1)} %iota_xor_fusion.me_ref.order_ref, f32[42,16,128]{2,1,0:T(8,128)S(1)} %get-tuple-element.10.refs_0_, f32[42,16,128]{2,1,0:T(8,128)S(1)} %collective-permute-done.refs_1_, f32[42,16,128]{2,1,0:T(8,128)S(1)} %collective-permute-done.1.refs_2_, ...), custom_call_target="tpu_custom_call" | custom-call | tf_op jit(solution)/shard_map/line_tiles/pallas_call | solution.py:213
  51.3 2.6 %all-to-all-start.1 = ((f32[32,8,128]{2,1,0:T(8,128)}), f32[32,8,128]{2,1,0:T(8,128)S(1)}, u32[]{:S(2)}, u32[]{:S(2)}) async-start(f32[32,8,128]{2,1,0:T(8,128)} %line_tiles.1), calls=%async_computation.1 | async-start | bytes 262144 | tf_op jit(solution)/shard_map/all_to_all | solution.py:296
  53.9 0.7 %copy.6 = f32[33,16]{0,1:T(8,128)} copy(f32[33,16]{1,0:T(8,128)S(1)} %get-tuple-element.14) | data formatting | bytes 4224
  54.5 7.6 %all-to-all-done.1.tiles_ref = f32[32,8,128]{2,1,0:T(8,128)S(1)} async-done(((f32[32,8,128]{2,1,0:T(8,128)}), f32[32,8,128]{2,1,0:T(8,128)S(1)}, u32[]{:S(2)}, u32[]{:S(2)}) %all-to-all-start.1) | async-done | bytes 131104 | tf_op jit(solution)/shard_map/all_to_all | solution.py:296
  62.1 0.2 own_block.1
  62.3 0.7 %copy.7 = f32[42,21]{0,1:T(8,128)} copy(f32[42,21]{1,0:T(8,128)S(1)} %own_block.1) | data formatting | bytes 7056
  (2 shorter events, 0.0 us)
Async XLA Ops:
  2.7 11.7 %copy-start = (f32[33,16]{0,1:T(8,128)S(1)}, f32[33,16]{0,1:T(8,128)}, u32[]{:S(2)}) copy-start(f32[33,16]{0,1:T(8,128)} %param.3) | copy-start | bytes 6340
  7.2 15.5 %all-to-all-start = ((f32[32,8,128]{2,1,0:T(8,128)}), f32[32,8,128]{2,1,0:T(8,128)S(1)}, u32[]{:S(2)}, u32[]{:S(2)}) async-start(f32[32,8,128]{2,1,0:T(8,128)} %gram_tiles.1), calls=%async_computation | async-start | bytes 262144 | tf_op jit(solution)/shard_map/all_to_all | solution.py:266
  30.4 11.0 %collective-permute-start = (f32[42,16,128]{2,1,0:T(8,128)S(1)}, f32[42,16,128]{2,1,0:T(8,128)S(1)}, u32[]{:S(2)}, u32[]{:S(2)}) collective-permute-start(f32[42,16,128]{2,1,0:T(8,128)S(1)} %get-tuple-element.11), channel_id=1, source_target_pairs={{0,2},{2,0},{4,6},{6,4},{1,3},{3,1},{5,7},{7,5},{8,10},{10,8},{12,... | collective-permute-start | bytes 1032200 | tf_op jit(solution)/shard_map/ppermute | solution.py:247
  30.9 17.2 %collective-permute-start.1 = (f32[42,16,128]{2,1,0:T(8,128)S(1)}, f32[42,16,128]{2,1,0:T(8,128)S(1)}, u32[]{:S(2)}, u32[]{:S(2)}) collective-permute-start(f32[42,16,128]{2,1,0:T(8,128)S(1)} %get-tuple-element.12), channel_id=1, source_target_pairs={{0,4},{2,6},{4,0},{6,2},{1,5},{3,7},{5,1},{7,3},{8,12},{10,14},{12... | collective-permute-start | bytes 1032200 | tf_op jit(solution)/shard_map/ppermute | solution.py:247
  31.9 16.2 %collective-permute-start.2 = (f32[42,16,128]{2,1,0:T(8,128)S(1)}, f32[42,16,128]{2,1,0:T(8,128)S(1)}, u32[]{:S(2)}, u32[]{:S(2)}) collective-permute-start(f32[42,16,128]{2,1,0:T(8,128)S(1)} %get-tuple-element.13), channel_id=1, source_target_pairs={{0,6},{2,4},{4,2},{6,0},{1,7},{3,5},{5,3},{7,1},{8,14},{10,12},{12... | collective-permute-start | bytes 1032200 | tf_op jit(solution)/shard_map/ppermute | solution.py:247
  51.3 10.8 %all-to-all-start.1 = ((f32[32,8,128]{2,1,0:T(8,128)}), f32[32,8,128]{2,1,0:T(8,128)S(1)}, u32[]{:S(2)}, u32[]{:S(2)}) async-start(f32[32,8,128]{2,1,0:T(8,128)} %line_tiles.1), calls=%async_computation.1 | async-start | bytes 262144 | tf_op jit(solution)/shard_map/all_to_all | solution.py:296

commit v2 on v1

v2 whole, which is shorter than its diff:
```python
import functools
import math

import jax
import jax.numpy as jnp
from jax import lax
from jax.experimental import pallas as pl
from jax.experimental.pallas import tpu as pltpu
from jax.sharding import PartitionSpec as P

ITERS = 4
LANES = 128
ROWS = 8
HALF_ROWS = 16
HIGH = lax.Precision.HIGHEST
BY_LAST = (((1,), (1,)), ((), ()))
PLAIN = (((1,), (0,)), ((), ()))
ALL = ("gx", "gy", "sa")
VMEM = pl.BlockSpec(memory_space=pltpu.VMEM)
ANY = pl.BlockSpec(memory_space=pl.ANY)
SMALL = pltpu.CompilerParams(vmem_limit_bytes=4 * 2**20)
PARAMS = pltpu.CompilerParams(vmem_limit_bytes=16 * 2**20)
MIDDLE = pltpu.CompilerParams(vmem_limit_bytes=32 * 2**20)
LARGE = pltpu.CompilerParams(vmem_limit_bytes=61 * 2**20)


def lasting(time):
    return pl.CostEstimate(flops=0, bytes_accessed=int(time * 3.5e6), transcendentals=0)


def partner(k):
    return jnp.bitwise_xor(lax.axis_index("gy"), k)


def up(value, step):
    return -(-value // step) * step


def split(value):
    high = value.astype(jnp.bfloat16)
    low = (value - high.astype(jnp.float32)).astype(jnp.bfloat16)
    return high, low


def dot32(left, right, dims):
    return lax.dot_general(left, right, dims, preferred_element_type=jnp.float32)


def triangle(species):
    places, at = [], 0
    for top in range(0, species, ROWS):
        places.append((top, at))
        at += species - top
    return places


def stacked(rows, pitch):
    species, lines, cells = rows.shape
    high, low = split(rows.reshape(species, lines * cells))
    blank = jnp.zeros((pitch - species, lines * cells), jnp.bfloat16)
    return jnp.concatenate([high, blank, low, blank], axis=0)


def gram_kernel(cuts, cells_x, field_ref, tiles_ref, *refs):
    early_refs, (buffer, early, total, sems) = refs[:-4], refs[-4:]
    species = field_ref.shape[0]
    pitch = up(species, HALF_ROWS)
    spans = [slice(top, end) for top, end in zip(cuts[:-1], cuts[1:], strict=True)]
    copies = [
        pltpu.make_async_copy(field_ref.at[:, span, :], buffer.at[:, span, :], sems.at[i])
        for i, span in enumerate(spans)
    ]
    for copy in copies:
        copy.start()
    total[...] = jnp.zeros_like(total)
    sends = [
        pltpu.make_async_copy(early.at[k], ref, sems.at[len(copies) + k])
        for k, ref in enumerate(early_refs)
    ]
    for i, (copy, span) in enumerate(zip(copies, spans, strict=True)):
        copy.wait()
        for k, send in enumerate(sends if i == 0 else ()):
            early[k] = buffer[:, pl.ds(partner(partners(len(sends))[k]), early.shape[2], stride=cells_x), :]
            send.start()
        both = stacked(buffer[:, span, :], pitch)
        total[: 2 * pitch, : 2 * pitch] += dot32(both, both, BY_LAST)
    upper = total[:pitch, :] + total[pitch : 2 * pitch, :]
    upper = upper + pltpu.roll(upper, LANES - pitch, 1)
    lane = lax.broadcasted_iota(jnp.int32, (ROWS, LANES), 1)
    tile = jnp.zeros((ROWS, LANES), jnp.float32)
    for top, at in triangle(species):
        moved = pltpu.roll(upper[top : top + ROWS, :], (at - top) % LANES, 1)
        tile = jnp.where((lane >= at) & (lane < at + species - top), moved, tile)
    tiles_ref[...] = jnp.broadcast_to(tile[None], tiles_ref.shape)
    for send in sends:
        send.wait()


def by_rows(field):
    species, cells_x, lines, cells = field.shape
    return field.transpose(0, 2, 1, 3).reshape(species, lines * cells_x, cells)


def gram_tiles(field, devices, early, count):
    species, cells_x, lines, cells = field.shape
    rows = lines * cells_x
    pitch = up(species, HALF_ROWS)
    cuts = (0, max(up(rows * 2 // 5, ROWS), early * cells_x), up(rows * 3 // 4, ROWS), rows)
    return pl.pallas_call(
        functools.partial(gram_kernel, cuts, cells_x),
        in_specs=[ANY],
        out_specs=[VMEM] + [ANY] * count,
        out_shape=[jax.ShapeDtypeStruct((devices, ROWS, LANES), jnp.float32)]
        + [jax.ShapeDtypeStruct((species, early, cells), jnp.float32)] * count,
        scratch_shapes=[
            pltpu.VMEM((species, rows, cells), jnp.float32),
            pltpu.VMEM((max(count, 1), species, max(early, ROWS), cells), jnp.float32),
            pltpu.VMEM((up(2 * pitch, LANES), LANES), jnp.float32),
            pltpu.SemaphoreType.DMA((len(cuts) - 1 + count,)),
        ],
        compiler_params=LARGE,
        name="gram_tiles",
    )(by_rows(field))


def orth(rows):
    ranks = rows.shape[0]
    inner = lax.dot_general(rows, rows, BY_LAST, precision=HIGH, preferred_element_type=jnp.float32)
    columns = [jnp.broadcast_to(inner[:, k : k + 1], (ranks, LANES)) for k in range(ranks)]
    index = lax.broadcasted_iota(jnp.int32, (ranks, LANES), 0)
    pivots = jnp.ones((ranks, LANES), jnp.float32)
    for k in range(ranks):
        pivot = columns[k][k : k + 1, :]
        factor = jnp.where(index > k, columns[k] * (1.0 / pivot), 0.0)
        pivots = jnp.where(index == k, pivot, pivots)
        for j in range(k + 1, ranks):
            columns[j] = columns[j] - factor * columns[j][k : k + 1, :]
        rows = rows - factor * rows[k : k + 1, :]
    return rows * lax.rsqrt(pivots)


def start_kernel(start_ref, out_ref):
    out_ref[...] = orth(orth(start_ref[...]))


def unpacked(tile, species):
    parts = [pltpu.roll(tile, (top - at) % LANES, 1) for top, at in triangle(species)]
    parts += [jnp.zeros((ROWS, LANES), jnp.float32)] * (LANES // ROWS - len(parts))
    upper = jnp.concatenate(parts, axis=0)
    row = lax.broadcasted_iota(jnp.int32, (LANES, LANES), 0)
    column = lax.broadcasted_iota(jnp.int32, (LANES, LANES), 1)
    gram = jnp.where(column >= row // ROWS * ROWS, upper, upper.T)
    return jnp.where((row < species) & (column < species), gram, 0.0)


def turn(rows, gram):
    return orth(orth(jnp.dot(rows, gram, precision=HIGH, preferred_element_type=jnp.float32)))


def doubled(rows, pitch):
    high, low = split(rows[:, :pitch])
    both = jnp.concatenate([high, low], axis=0)
    return jnp.concatenate([both, both], axis=1)


def projected(left, stack):
    both = dot32(left, stack, PLAIN)
    ranks = left.shape[0] // 2
    return both[:ranks] + both[ranks:]


def whole_call(kernel, out_shape, name, *args):
    return pl.pallas_call(
        kernel, out_shape=out_shape, compiler_params=SMALL, cost_estimate=lasting(0), name=name
    )(*args)


def basis_kernel(species, scale, tiles_ref, start_ref, rows_ref, basis_ref):
    gram = unpacked(jnp.sum(tiles_ref[...], axis=0) * scale, species)
    rows = start_ref[...]
    for _ in range(ITERS):
        rows = turn(rows, gram)
    rows_ref[...] = rows
    basis_ref[...] = rows[:, :species]


def basis_late_kernel(scale, top, cells_x, tiles_ref, start_ref, field_ref, *refs):
    rows_ref, basis_ref = refs[:2]
    late_refs, (buffer, core_ref, sem) = refs[2:-3], refs[-3:]
    species, _, cells = field_ref.shape
    pitch = up(species, HALF_ROWS)
    copy = pltpu.make_async_copy(field_ref.at[:, top:, :], buffer, sem)
    copy.start()
    gram = unpacked(jnp.sum(tiles_ref[...], axis=0) * scale, species)
    rows = start_ref[...]
    for _ in range(ITERS - 1):
        rows = turn(rows, gram)
    copy.wait()
    stack = stacked(buffer[...], pitch)
    rows = turn(rows, gram)
    rows_ref[...] = rows
    basis_ref[...] = rows[:, :species]
    core = projected(doubled(rows, pitch), stack)
    for i in range(core_ref.shape[0]):
        core_ref[i] = core[:, i * cells : (i + 1) * cells]
    for k, late_ref in zip(partners(len(late_refs)), late_refs, strict=True):
        for y in range(late_ref.shape[0]):
            late_ref[y] = core_ref[y * cells_x + partner(k)]


def basis_late(scale, early, count, tiles, first, field):
    species, cells_x, lines, cells = field.shape
    ranks = first.shape[0]
    late = lines - early
    return pl.pallas_call(
        functools.partial(basis_late_kernel, scale, early * cells_x, cells_x),
        in_specs=[VMEM, VMEM, ANY],
        out_specs=[VMEM] * (2 + count),
        out_shape=[
            jax.ShapeDtypeStruct((ranks, LANES), jnp.float32),
            jax.ShapeDtypeStruct((ranks, species), jnp.float32),
        ]
        + [jax.ShapeDtypeStruct((late, ranks, cells), jnp.float32)] * count,
        scratch_shapes=[
            pltpu.VMEM((species, late * cells_x, cells), jnp.float32),
            pltpu.VMEM((late * cells_x, ranks, cells), jnp.float32),
            pltpu.SemaphoreType.DMA,
        ],
        compiler_params=MIDDLE,
        cost_estimate=lasting(30),
        name="basis_late",
    )(tiles, first, by_rows(field))


def place(core, at, high_ref, low_ref):
    lines, ranks, cells = core.shape
    block = core.reshape(lines, ranks * cells)
    if lines % HALF_ROWS:
        fill = jnp.zeros((up(lines, HALF_ROWS) - lines, ranks * cells), jnp.float32)
        block = jnp.concatenate([block, fill], axis=0)
    high, low = split(block)
    high_ref[pl.ds(at, block.shape[0]), :] = high
    low_ref[pl.ds(at, block.shape[0]), :] = low


def ready_kernel(rows_ref, late_ref, *refs):
    pieces, (high_ref, low_ref, part_ref) = refs[:-3], refs[-3:]
    pitch = high_ref.shape[0] // len(pieces)
    species, early, cells = pieces[0].shape
    wide = up(species, HALF_ROWS)
    left = doubled(rows_ref[...], wide)
    for k, piece in zip(partners(len(pieces)), pieces, strict=True):
        core = projected(left, stacked(piece[...], wide))
        for y in range(early):
            part_ref[y] = core[:, y * cells : (y + 1) * cells]
        place(part_ref[...], pl.multiple_of(partner(k) * pitch, HALF_ROWS), high_ref, low_ref)
    at = pl.multiple_of(partner(0) * pitch + early, HALF_ROWS)
    place(late_ref[...], at, high_ref, low_ref)


def ready_rows(rows, own, pieces, lines):
    species, early, cells = pieces[0].shape
    ranks = rows.shape[0]
    shape = (len(pieces) * up(lines, HALF_ROWS), ranks * cells)
    return pl.pallas_call(
        ready_kernel,
        in_specs=[VMEM] * (2 + len(pieces)),
        out_specs=[VMEM, VMEM],
        out_shape=[jax.ShapeDtypeStruct(shape, jnp.bfloat16)] * 2,
        scratch_shapes=[pltpu.VMEM((early, ranks, cells), jnp.float32)],
        compiler_params=PARAMS,
        name="ready_rows",
    )(rows, own, *pieces)


def packing(lines, columns):
    groups = LANES // lines
    deep = -(-columns // groups)
    return groups, deep, up(deep, ROWS)


def line_kernel(axes, lines, early, count, *refs):
    n_gx, n_gy, n_sa = axes
    pieces, ready, (out_ref, high_ref, low_ref, gram_ref) = refs[:count], refs[count:-4], refs[-4:]
    pitch = high_ref.shape[0] // n_gy
    if ready:
        high_ref[...] = ready[0][...]
        low_ref[...] = ready[1][...]
    for k in range(count):
        block = partner(partners(n_gy)[n_gy - count + k])
        place(pieces[k][...], pl.multiple_of(block * pitch + early, HALF_ROWS), high_ref, low_ref)
    size = n_gy * pitch
    gram_ref[...] = jnp.zeros_like(gram_ref)
    gram_ref[:size, :size] = dot32(high_ref[...], low_ref[...], BY_LAST)
    cross = gram_ref[:size, :size]
    gram_ref[:size, :size] = dot32(high_ref[...], high_ref[...], BY_LAST) + cross + cross.T
    wide = gram_ref.shape[1]
    columns = lines * n_gy // (n_gx * n_sa)
    groups, deep, tall = packing(lines, columns)
    lane = lax.broadcasted_iota(jnp.int32, (tall, LANES), 1)
    for c in range(n_gx * n_sa):
        first = c * columns
        base = first // lines * pitch + first % lines
        bands = [gram_ref[base + g * deep : base + g * deep + tall, :] for g in range(groups)]
        for i in range(n_gy):
            tile = jnp.zeros((tall, LANES), jnp.float32)
            for g in range(groups):
                moved = pltpu.roll(bands[g], (g * lines - i * pitch) % wide, 1)[:, :LANES]
                tile = jnp.where((lane >= g * lines) & (lane < (g + 1) * lines), moved, tile)
            out_ref[((c // n_sa) * n_gy + i) * n_sa + c % n_sa] = tile


def line_tiles(pieces, ready, axes, lines, early):
    n_gx, n_gy, n_sa = axes
    _, ranks, cells = pieces[0].shape
    size = n_gy * up(lines, HALF_ROWS)
    _, _, tall = packing(lines, lines * n_gy // (n_gx * n_sa))
    return pl.pallas_call(
        functools.partial(line_kernel, axes, lines, early, len(pieces)),
        in_specs=[VMEM] * (len(pieces) + len(ready)),
        out_specs=VMEM,
        out_shape=jax.ShapeDtypeStruct((n_gx * n_gy * n_sa, tall, LANES), jnp.float32),
        scratch_shapes=[
            pltpu.VMEM((size, ranks * cells), jnp.bfloat16),
            pltpu.VMEM((size, ranks * cells), jnp.bfloat16),
            pltpu.VMEM((size + tall, up(size, LANES)), jnp.float32),
        ],
        compiler_params=PARAMS,
        name="line_tiles",
    )(*pieces, *ready)


def block_kernel(scale, tiles_ref, out_ref):
    columns, lines = out_ref.shape
    groups, deep, _ = packing(lines, columns)
    tile = jnp.sum(tiles_ref[...], axis=0) * scale
    for g in range(groups):
        part = tile if g == 0 else pltpu.roll(tile, LANES - g * lines, 1)
        high = min(deep, columns - g * deep)
        if high > 0:
            out_ref[g * deep : g * deep + high, :] = part[:high, :lines]


def partners(size):
    if size & (size - 1):
        raise ValueError("axis size")
    return sorted(range(size), key=lambda k: (k > 0, -k.bit_count(), k))


def exchanges(pieces, size):
    return pieces[:1] + [
        lax.ppermute(piece, "gy", [(a, a ^ k) for a in range(size)])
        for k, piece in zip(partners(size)[1:], pieces[1:], strict=True)
    ]


def on_device(field, start):
    species, cells_x, lines, cells_z = field.shape
    ranks = start.shape[1]
    n_gx, n_gy, n_sa = lax.axis_size("gx"), lax.axis_size("gy"), lax.axis_size("sa")
    axes, devices = (n_gx, n_gy, n_sa), n_gx * n_gy * n_sa
    total_x, total_y, total_z = cells_x * n_gx, lines * n_gy, cells_z * n_sa
    columns = total_y // (n_gx * n_sa)
    me = lax.axis_index("gy")
    parts_x = math.gcd(n_gy, cells_x)
    parts_z = n_gy // parts_x
    early = lines * 2 // 5 // HALF_ROWS * HALF_ROWS
    by_x = parts_x == cells_x and parts_z == 1 and early > 0
    early = early if by_x else 0

    tiles, *outgoing = gram_tiles(field, devices, early, n_gy if by_x else 0)
    tiles = lax.all_to_all(tiles, ALL, 0, 0, tiled=True)
    first = whole_call(
        start_kernel,
        jax.ShapeDtypeStruct((ranks, LANES), jnp.float32),
        "start_rows",
        jnp.pad(start.T, ((0, 0), (0, LANES - species))),
    )
    scale = 1.0 / (total_x * total_y * total_z)
    if by_x:
        received = exchanges(outgoing, n_gy)
        rows, basis, own, *pieces = basis_late(scale, early, n_gy, tiles, first, field)
        own, *pieces = exchanges([own, *pieces], n_gy)
        ready = ready_rows(rows, own, received, lines)
    else:
        rows, basis = whole_call(
            functools.partial(basis_kernel, species, scale),
            [
                jax.ShapeDtypeStruct((ranks, LANES), jnp.float32),
                jax.ShapeDtypeStruct((ranks, species), jnp.float32),
            ],
            "basis_rows",
            tiles,
            first,
        )
        wide_x, wide_z = cells_x // parts_x, cells_z // parts_z
        core = jnp.einsum("rs,sxyz->yrxz", rows[:, :species], field, precision=HIGH)
        pieces, ready = [], []
        for k in partners(n_gy):
            at = jnp.bitwise_xor(me, k)
            cut = lax.dynamic_slice(
                core,
                (0, 0, at // parts_z * wide_x, at % parts_z * wide_z),
                (lines, ranks, wide_x, wide_z),
            )
            pieces.append(cut.reshape(lines, -1, LANES))
        pieces = exchanges(pieces, n_gy)
    blocks = line_tiles(pieces, ready, axes, lines, early)
    blocks = lax.all_to_all(blocks, ALL, 0, 0, tiled=True)
    block = whole_call(
        functools.partial(block_kernel, 1.0 / (ranks * total_x * total_z)),
        jax.ShapeDtypeStruct((columns, lines), jnp.float32),
        "own_block",
        blocks,
    )
    return (basis.T, block.T)


def solution(mesh):
    in_specs = (P(None, "gx", "gy", "sa"), P())
    out_specs = (P(), P("gy", ("gx", "sa")))
    return jax.shard_map(
        on_device, mesh=mesh, in_specs=in_specs, out_specs=out_specs, check_vma=False
    )
```

time: 63.3 us -> 51.5 us (0.81)
  waiting for transfers between devices: 29.1 us -> 11.7 us
  blocking collectives: 0 us -> 10.6 us
  local copies, waits for them, and re-layouts: 3.47 us -> 0.02 us
  Pallas kernels: 16.3 us -> 13.4 us
  starting transfers between devices: 13.4 us -> 14.8 us
    all_to_all x2 -> x1, waiting for transfers between devices: 14.9 us -> 4.2 us  [on_device(): tiles = lax.all_to_all(tiles, ALL, 0, 0, tiled=True)]
    all_to_all x0 -> x1, blocking collectives: none -> 10.6 us  [on_device(): blocks = lax.all_to_all(blocks, ALL, 0, 0, tiled=True)]
    ppermute x3 -> x6, starting transfers between devices: 3.55 us -> 10.8 us  [exchanges(): lax.ppermute(piece, 'gy', [(a, a ^ k) for a in range(size)])]
    ppermute x3 -> x6, waiting for transfers between devices: 14.1 us -> 7.47 us  [exchanges(): lax.ppermute(piece, 'gy', [(a, a ^ k) for a in range(size)])]
    all_to_all x2 -> x1, starting transfers between devices: 9.9 us -> 3.96 us  [on_device(): tiles = lax.all_to_all(tiles, ALL, 0, 0, tiled=True)]
    unnamed x5 -> x6, local copies, waits for them, and re-layouts: 3.46 us -> 0.01 us
    pallas_call x6, Pallas kernels: 16.3 us -> 13.4 us  [the longest x1 4.94 us: basis_late(): pl.pallas_call(functools.partial(basis_late_kernel, scale, early * cells_...]
  transfers between devices with their start and end apart: 5 -> 7, of which waited for: 4 -> 4; matrix products, arithmetic and copies ran while one was open for 1% -> 0% of each run, Pallas kernels for 1% -> 15%
where the time goes in v2:
time: 51.5 us; the launch traced here: 51.2 us
  starting transfers between devices  14.8 us (29%)
  Pallas kernels  13.4 us (26%)
  waiting for transfers between devices  11.7 us (23%)
  blocking collectives  10.6 us (21%)
  between operations  0.71 us (1%)
    ppermute x6, starting transfers between devices, exchanges(): lax.ppermute(piece, 'gy', [(a, a ^ k) for a in range(size)])  10.8 us
    all_to_all x1, blocking collectives, on_device(): blocks = lax.all_to_all(blocks, ALL, 0, 0, tiled=True)  10.6 us
    ppermute x6, waiting for transfers between devices, exchanges(): lax.ppermute(piece, 'gy', [(a, a ^ k) for a in range(size)])  7.47 us
    pallas_call x1, Pallas kernels, basis_late(): pl.pallas_call(functools.partial(basis_late_kernel, scale, early * cells_...  4.94 us
    all_to_all x1, waiting for transfers between devices, on_device(): tiles = lax.all_to_all(tiles, ALL, 0, 0, tiled=True)  4.2 us
    pallas_call x1, Pallas kernels, gram_tiles(): pl.pallas_call(functools.partial(gram_kernel, cuts, cells_x), in_specs=[A...  3.97 us
    all_to_all x1, starting transfers between devices, on_device(): tiles = lax.all_to_all(tiles, ALL, 0, 0, tiled=True)  3.96 us
    pallas_call x1, Pallas kernels, ready_rows(): pl.pallas_call(ready_kernel, in_specs=[VMEM] * (2 + len(pieces)), out_spe...  1.76 us
  transfers between devices with their start and end apart: 7, of which 4 were waited for; matrix products, arithmetic and copies ran while one was open for 0% of the time, Pallas kernels for 15%

profile of v2, /device:TPU:0, one launch (start us, length us, event | category | flops | bytes accessed | tf_op | source)
XLA Modules:
  0.0 51.2 jit_solution(2625334017104060915)
XLA Ops:
  0.6 0.0 copy-start
  0.6 0.0 copy-start.2
  0.6 4.0 %gram_tiles.1 = (f32[32,8,128]{2,1,0:T(8,128)}, f32[33,16,128]{2,1,0:T(8,128)}, f32[33,16,128]{2,1,0:T(8,128)}, f32[33,16,128]{2,1,0:T(8,128)}, f32[33,16,128]{2,1,0:T(8,128)}) custom-call(f32[33,168,128]{2,1,0:T(8,128)} %bitcast.6), custom_call_target="tpu_custom_call" | custom-call | tf_op jit(solution)/shard_map/gram_tiles/pallas_call | solution.py:109
  4.6 0.0 copy-start.1
  4.6 4.0 %collective-permute-start.3 = (f32[33,16,128]{2,1,0:T(8,128)}, f32[33,16,128]{2,1,0:T(8,128)}, u32[]{:S(2)}, u32[]{:S(2)}) collective-permute-start(f32[33,16,128]{2,1,0:T(8,128)} %get-tuple-element.23), channel_id=1, source_target_pairs={{0,6},{2,4},{4,2},{6,0},{1,7},{3,5},{5,3},{7,1},{8,14},{10,12},{12... | collective-permute-start | bytes 811016 | tf_op jit(solution)/shard_map/ppermute | solution.py:352
  8.6 4.0 %all-to-all-start = ((f32[32,8,128]{2,1,0:T(8,128)}), f32[32,8,128]{2,1,0:T(8,128)S(1)}, u32[]{:S(2)}, u32[]{:S(2)}) async-start(f32[32,8,128]{2,1,0:T(8,128)} %get-tuple-element.15), calls=%async_computation | async-start | bytes 262144 | tf_op jit(solution)/shard_map/all_to_all | solution.py:372
  12.6 1.8 %collective-permute-start.4 = (f32[33,16,128]{2,1,0:T(8,128)}, f32[33,16,128]{2,1,0:T(8,128)}, u32[]{:S(2)}, u32[]{:S(2)}) collective-permute-start(f32[33,16,128]{2,1,0:T(8,128)} %get-tuple-element.24), channel_id=1, source_target_pairs={{0,2},{2,0},{4,6},{6,4},{1,3},{3,1},{5,7},{7,5},{8,10},{10,8},{12,... | collective-permute-start | bytes 811016 | tf_op jit(solution)/shard_map/ppermute | solution.py:352
  14.4 1.5 %collective-permute-start.5 = (f32[33,16,128]{2,1,0:T(8,128)}, f32[33,16,128]{2,1,0:T(8,128)}, u32[]{:S(2)}, u32[]{:S(2)}) collective-permute-start(f32[33,16,128]{2,1,0:T(8,128)} %get-tuple-element.25), channel_id=1, source_target_pairs={{0,4},{2,6},{4,0},{6,2},{1,5},{3,7},{5,1},{7,3},{8,12},{10,14},{12... | collective-permute-start | bytes 811016 | tf_op jit(solution)/shard_map/ppermute | solution.py:352
  15.9 0.0 copy-done.2
  15.9 0.8 %start_rows.1.start_ref = f32[16,128]{1,0:T(8,128)S(1)} custom-call(f32[16,128]{1,0:T(8,128)S(1)} %pad.4.start_ref), custom_call_target="tpu_custom_call" | custom-call | tf_op jit(solution)/shard_map/start_rows/pallas_call | solution.py:173
  16.7 4.2 %all-to-all-done.tiles_ref = f32[32,8,128]{2,1,0:T(8,128)S(1)} async-done(((f32[32,8,128]{2,1,0:T(8,128)}), f32[32,8,128]{2,1,0:T(8,128)S(1)}, u32[]{:S(2)}, u32[]{:S(2)}) %all-to-all-start) | async-done | bytes 131104 | tf_op jit(solution)/shard_map/all_to_all | solution.py:372
  20.9 0.0 copy-done
  20.9 4.9 %basis_late.1 = (f32[16,128]{1,0:T(8,128)S(1)}, f32[16,33]{1,0:T(8,128)}, f32[26,16,128]{2,1,0:T(8,128)S(1)}, f32[26,16,128]{2,1,0:T(8,128)S(1)}, f32[26,16,128]...) custom-call(f32[32,8,128]{2,1,0:T(8,128)S(1)} %all-to-all-done.tiles_ref, f32[16,128]{1,0:T(8,128)S(1)} %start_rows.1.start_ref, ...), custom_call_target="tpu_custom_call" | custom-call | bytes 105000000 | tf_op jit(solution)/shard_map/basis_late/pallas_call | solution.py:215
  25.9 0.9 %collective-permute-start = (f32[26,16,128]{2,1,0:T(8,128)S(1)}, f32[26,16,128]{2,1,0:T(8,128)S(1)}, u32[]{:S(2)}, u32[]{:S(2)}) collective-permute-start(f32[26,16,128]{2,1,0:T(8,128)S(1)} %get-tuple-element.17), channel_id=1, source_target_pairs={{0,6},{2,4},{4,2},{6,0},{1,7},{3,5},{5,3},{7,1},{8,14},{10,12},{12... | collective-permute-start | bytes 638984 | tf_op jit(solution)/shard_map/ppermute | solution.py:352
  26.7 1.4 %collective-permute-start.1 = (f32[26,16,128]{2,1,0:T(8,128)S(1)}, f32[26,16,128]{2,1,0:T(8,128)S(1)}, u32[]{:S(2)}, u32[]{:S(2)}) collective-permute-start(f32[26,16,128]{2,1,0:T(8,128)S(1)} %get-tuple-element.18), channel_id=1, source_target_pairs={{0,2},{2,0},{4,6},{6,4},{1,3},{3,1},{5,7},{7,5},{8,10},{10,8},{12,... | collective-permute-start | bytes 638984 | tf_op jit(solution)/shard_map/ppermute | solution.py:352
  28.1 0.0 collective-permute-done.3.refs_1_
  28.1 1.3 %collective-permute-start.2 = (f32[26,16,128]{2,1,0:T(8,128)S(1)}, f32[26,16,128]{2,1,0:T(8,128)S(1)}, u32[]{:S(2)}, u32[]{:S(2)}) collective-permute-start(f32[26,16,128]{2,1,0:T(8,128)S(1)} %get-tuple-element.19), channel_id=1, source_target_pairs={{0,4},{2,6},{4,0},{6,2},{1,5},{3,7},{5,1},{7,3},{8,12},{10,14},{12... | collective-permute-start | bytes 638984 | tf_op jit(solution)/shard_map/ppermute | solution.py:352
  29.4 0.0 collective-permute-done.4.refs_2_
  29.4 0.0 collective-permute-done.5.refs_3_
  29.4 0.0 copy-done.1
  29.4 1.8 %ready_rows.1 = (bf16[192,2048]{1,0:T(8,128)(2,1)S(1)}, bf16[192,2048]{1,0:T(8,128)(2,1)S(1)}) custom-call(f32[16,128]{1,0:T(8,128)S(1)} %get-tuple-element.20.rows_ref, f32[26,16,128]{2,1,0:T(8,128)S(1)} %get-tuple-element.21.late_ref, f32[33,16,128]{2,1,0:T(8,128)S(1)} %copy-done.1, f32[33,16,128]{2,1,0:T(8,128)} %collective-permute-done.3.refs_1_, ...), custom_call_target="tpu_custom_call" | custom-call | tf_op jit(solution)/shard_map/ready_rows/pallas_call | solution.py:265
  31.2 3.8 %collective-permute-done.refs_0_ = f32[26,16,128]{2,1,0:T(8,128)S(1)} collective-permute-done((f32[26,16,128]{2,1,0:T(8,128)S(1)}, f32[26,16,128]{2,1,0:T(8,128)S(1)}, u32[]{:S(2)}, u32[]{:S(2)}) %collective-permute-start) | collective-permute-done | bytes 213024 | tf_op jit(solution)/shard_map/ppermute | solution.py:352
  35.0 2.6 %collective-permute-done.1.refs_1_ = f32[26,16,128]{2,1,0:T(8,128)S(1)} collective-permute-done((f32[26,16,128]{2,1,0:T(8,128)S(1)}, f32[26,16,128]{2,1,0:T(8,128)S(1)}, u32[]{:S(2)}, u32[]{:S(2)}) %collective-permute-start.1) | collective-permute-done | bytes 213024 | tf_op jit(solution)/shard_map/ppermute | solution.py:352
  37.5 1.1 %collective-permute-done.2.refs_2_ = f32[26,16,128]{2,1,0:T(8,128)S(1)} collective-permute-done((f32[26,16,128]{2,1,0:T(8,128)S(1)}, f32[26,16,128]{2,1,0:T(8,128)S(1)}, u32[]{:S(2)}, u32[]{:S(2)}) %collective-permute-start.2) | collective-permute-done | bytes 213024 | tf_op jit(solution)/shard_map/ppermute | solution.py:352
  38.7 1.2 %line_tiles.1 = f32[32,8,128]{2,1,0:T(8,128)S(1)} custom-call(f32[26,16,128]{2,1,0:T(8,128)S(1)} %collective-permute-done.refs_0_, f32[26,16,128]{2,1,0:T(8,128)S(1)} %collective-permute-done.1.refs_1_, f32[26,16,128]{2,1,0:T(8,128)S(1)} %collective-permute-done.2.refs_2_, bf16[192,2048]{1,0:T(8,128)(2,1)S(1)} %get-tuple-element.26.refs_3_, ...), custom_call_target="tpu_custom_call" | custom-call | tf_op jit(solution)/shard_map/line_tiles/pallas_call | solution.py:318
  39.9 10.6 %all_to_all.10.tiles_ref = f32[32,8,128]{2,1,0:T(8,128)S(1)} all-to-all(f32[32,8,128]{2,1,0:T(8,128)S(1)} %line_tiles.1), channel_id=1, replica_groups=mesh['gx'=4,'gy'=4,'sa'=2] {'gx','gy','sa'}, dimensions={0} | all-to-all | bytes 262144 | tf_op jit(solution)/shard_map/all_to_all | solution.py:409
  50.5 0.7 %own_block.1 = f32[21,42]{1,0:T(8,128)} custom-call(f32[32,8,128]{2,1,0:T(8,128)S(1)} %all_to_all.10.tiles_ref), custom_call_target="tpu_custom_call" | custom-call | tf_op jit(solution)/shard_map/own_block/pallas_call | solution.py:173
  (1 shorter events, 0.0 us)
Async XLA Ops:
  0.6 20.3 %copy-start = (f32[33,4,42,128]{3,1,2,0:T(4,128)S(1)}, f32[33,4,42,128]{3,1,2,0:T(4,128)}, u32[]{:S(2)}) copy-start(f32[33,4,42,128]{3,1,2,0:T(4,128)} %param.2) | copy-start | bytes 8515588
  0.6 15.2 %copy-start.2 = (f32[33,16]{0,1:T(8,128)S(1)}, f32[33,16]{0,1:T(8,128)}, u32[]{:S(2)}) copy-start(f32[33,16]{0,1:T(8,128)} %param.3) | copy-start | bytes 6340
  4.6 24.8 %copy-start.1 = (f32[33,16,128]{2,1,0:T(8,128)S(1)}, f32[33,16,128]{2,1,0:T(8,128)}, u32[]{:S(2)}) copy-start(f32[33,16,128]{2,1,0:T(8,128)} %get-tuple-element.22.refs_0_) | copy-start | bytes 811012
  4.6 23.4 %collective-permute-start.3 = (f32[33,16,128]{2,1,0:T(8,128)}, f32[33,16,128]{2,1,0:T(8,128)}, u32[]{:S(2)}, u32[]{:S(2)}) collective-permute-start(f32[33,16,128]{2,1,0:T(8,128)} %get-tuple-element.23), channel_id=1, source_target_pairs={{0,6},{2,4},{4,2},{6,0},{1,7},{3,5},{5,3},{7,1},{8,14},{10,12},{12... | collective-permute-start | bytes 811016 | tf_op jit(solution)/shard_map/ppermute | solution.py:352
  8.6 12.3 %all-to-all-start = ((f32[32,8,128]{2,1,0:T(8,128)}), f32[32,8,128]{2,1,0:T(8,128)S(1)}, u32[]{:S(2)}, u32[]{:S(2)}) async-start(f32[32,8,128]{2,1,0:T(8,128)} %get-tuple-element.15), calls=%async_computation | async-start | bytes 262144 | tf_op jit(solution)/shard_map/all_to_all | solution.py:372
  12.6 16.8 %collective-permute-start.4 = (f32[33,16,128]{2,1,0:T(8,128)}, f32[33,16,128]{2,1,0:T(8,128)}, u32[]{:S(2)}, u32[]{:S(2)}) collective-permute-start(f32[33,16,128]{2,1,0:T(8,128)} %get-tuple-element.24), channel_id=1, source_target_pairs={{0,2},{2,0},{4,6},{6,4},{1,3},{3,1},{5,7},{7,5},{8,10},{10,8},{12,... | collective-permute-start | bytes 811016 | tf_op jit(solution)/shard_map/ppermute | solution.py:352
  14.4 15.0 %collective-permute-start.5 = (f32[33,16,128]{2,1,0:T(8,128)}, f32[33,16,128]{2,1,0:T(8,128)}, u32[]{:S(2)}, u32[]{:S(2)}) collective-permute-start(f32[33,16,128]{2,1,0:T(8,128)} %get-tuple-element.25), channel_id=1, source_target_pairs={{0,4},{2,6},{4,0},{6,2},{1,5},{3,7},{5,1},{7,3},{8,12},{10,14},{12... | collective-permute-start | bytes 811016 | tf_op jit(solution)/shard_map/ppermute | solution.py:352
  25.9 9.1 %collective-permute-start = (f32[26,16,128]{2,1,0:T(8,128)S(1)}, f32[26,16,128]{2,1,0:T(8,128)S(1)}, u32[]{:S(2)}, u32[]{:S(2)}) collective-permute-start(f32[26,16,128]{2,1,0:T(8,128)S(1)} %get-tuple-element.17), channel_id=1, source_target_pairs={{0,6},{2,4},{4,2},{6,0},{1,7},{3,5},{5,3},{7,1},{8,14},{10,12},{12... | collective-permute-start | bytes 638984 | tf_op jit(solution)/shard_map/ppermute | solution.py:352
  26.7 10.8 %collective-permute-start.1 = (f32[26,16,128]{2,1,0:T(8,128)S(1)}, f32[26,16,128]{2,1,0:T(8,128)S(1)}, u32[]{:S(2)}, u32[]{:S(2)}) collective-permute-start(f32[26,16,128]{2,1,0:T(8,128)S(1)} %get-tuple-element.18), channel_id=1, source_target_pairs={{0,2},{2,0},{4,6},{6,4},{1,3},{3,1},{5,7},{7,5},{8,10},{10,8},{12,... | collective-permute-start | bytes 638984 | tf_op jit(solution)/shard_map/ppermute | solution.py:352
  28.1 10.6 %collective-permute-start.2 = (f32[26,16,128]{2,1,0:T(8,128)S(1)}, f32[26,16,128]{2,1,0:T(8,128)S(1)}, u32[]{:S(2)}, u32[]{:S(2)}) collective-permute-start(f32[26,16,128]{2,1,0:T(8,128)S(1)} %get-tuple-element.19), channel_id=1, source_target_pairs={{0,4},{2,6},{4,0},{6,2},{1,5},{3,7},{5,1},{7,3},{8,12},{10,14},{12... | collective-permute-start | bytes 638984 | tf_op jit(solution)/shard_map/ppermute | solution.py:352

commit v3 on v2

--- a/solution.py
+++ b/solution.py
@@ -125,18 +125,36 @@
 
 def orth(rows):
     ranks = rows.shape[0]
-    inner = lax.dot_general(rows, rows, BY_LAST, precision=HIGH, preferred_element_type=jnp.float32)
-    columns = [jnp.broadcast_to(inner[:, k : k + 1], (ranks, LANES)) for k in range(ranks)]
-    index = lax.broadcasted_iota(jnp.int32, (ranks, LANES), 0)
-    pivots = jnp.ones((ranks, LANES), jnp.float32)
+    blocks = ranks // ROWS
+    rows = [rows[b * ROWS : (b + 1) * ROWS] for b in range(blocks)]
+    shape = rows[0].shape
+    index = lax.broadcasted_iota(jnp.int32, shape, 0)
+    columns, pivots = [], []
     for k in range(ranks):
-        pivot = columns[k][k : k + 1, :]
-        factor = jnp.where(index > k, columns[k] * (1.0 / pivot), 0.0)
-        pivots = jnp.where(index == k, pivot, pivots)
+        row = rows[k // ROWS][k % ROWS : k % ROWS + 1, :]
+        columns.append(
+            {
+                b: jnp.broadcast_to(jnp.sum(rows[b] * row, axis=1, keepdims=True), shape)
+                for b in range(k // ROWS, blocks)
+            }
+        )
+    for k in range(ranks):
+        own, at = divmod(k, ROWS)
+        pivot = columns[k][own][at : at + 1, :]
+        below = {**columns[k], own: jnp.where(index > at, columns[k][own], 0.0)}
+        inverse = 1.0 / pivot
+        factor = {b: part * inverse for b, part in below.items()}
+        if at == 0:
+            pivots.append(jnp.broadcast_to(pivot, shape))
+        pivots[own] = jnp.where(index == at, pivot, pivots[own])
         for j in range(k + 1, ranks):
-            columns[j] = columns[j] - factor * columns[j][k : k + 1, :]
-        rows = rows - factor * rows[k : k + 1, :]
-    return rows * lax.rsqrt(pivots)
+            entry = columns[k][j // ROWS][j % ROWS : j % ROWS + 1, :]
+            for b in columns[j]:
+                columns[j][b] = columns[j][b] - factor[b] * entry
+        row = rows[own][at : at + 1, :]
+        for b in factor:
+            rows[b] = rows[b] - factor[b] * row
+    return jnp.concatenate([r * lax.rsqrt(p) for r, p in zip(rows, pivots, strict=True)], axis=0)
 
 
 def start_kernel(start_ref, out_ref):

time: 51.5 us -> 49.8 us (0.967)
  Pallas kernels: 13.4 us -> 11.4 us
    pallas_call x1, Pallas kernels: 4.94 us -> 3.28 us  [basis_late(): pl.pallas_call(functools.partial(basis_late_kernel, scale, early * cells_...]
  transfers between devices with their start and end apart: 7 -> 7, of which waited for: 4 -> 4; matrix products, arithmetic and copies ran while one was open for 0% -> 0% of each run, Pallas kernels for 15% -> 11%
where the time goes in v3:
time: 49.8 us; the launch traced here: 49.6 us
  starting transfers between devices  14.8 us (30%)
  waiting for transfers between devices  12.1 us (24%)
  Pallas kernels  11.4 us (23%)
  blocking collectives  10.6 us (21%)
  between operations  0.71 us (1%)
    ppermute x6, starting transfers between devices, exchanges(): lax.ppermute(piece, 'gy', [(a, a ^ k) for a in range(size)])  10.8 us
    all_to_all x1, blocking collectives, on_device(): blocks = lax.all_to_all(blocks, ALL, 0, 0, tiled=True)  10.6 us
    ppermute x6, waiting for transfers between devices, exchanges(): lax.ppermute(piece, 'gy', [(a, a ^ k) for a in range(size)])  7.47 us
    all_to_all x1, waiting for transfers between devices, on_device(): tiles = lax.all_to_all(tiles, ALL, 0, 0, tiled=True)  4.61 us
    pallas_call x1, Pallas kernels, gram_tiles(): pl.pallas_call(functools.partial(gram_kernel, cuts, cells_x), in_specs=[A...  3.97 us
    all_to_all x1, starting transfers between devices, on_device(): tiles = lax.all_to_all(tiles, ALL, 0, 0, tiled=True)  3.96 us
    pallas_call x1, Pallas kernels, basis_late(): pl.pallas_call(functools.partial(basis_late_kernel, scale, early * cells_...  3.28 us
    pallas_call x1, Pallas kernels, ready_rows(): pl.pallas_call(ready_kernel, in_specs=[VMEM] * (2 + len(pieces)), out_spe...  1.76 us
  transfers between devices with their start and end apart: 7, of which 4 were waited for; matrix products, arithmetic and copies ran while one was open for 0% of the time, Pallas kernels for 11%

profile of v3, /device:TPU:0, one launch (start us, length us, event | category | flops | bytes accessed | tf_op | source)
XLA Modules:
  0.0 49.6 jit_solution(17478578174025047830)
XLA Ops:
  0.6 0.0 copy-start
  0.6 0.0 copy-start.2
  0.6 4.0 %gram_tiles.1 = (f32[32,8,128]{2,1,0:T(8,128)}, f32[33,16,128]{2,1,0:T(8,128)}, f32[33,16,128]{2,1,0:T(8,128)}, f32[33,16,128]{2,1,0:T(8,128)}, f32[33,16,128]{2,1,0:T(8,128)}) custom-call(f32[33,168,128]{2,1,0:T(8,128)} %bitcast.6), custom_call_target="tpu_custom_call" | custom-call | tf_op jit(solution)/shard_map/gram_tiles/pallas_call | solution.py:109
  4.6 0.0 copy-start.1
  4.6 4.0 %collective-permute-start.3 = (f32[33,16,128]{2,1,0:T(8,128)}, f32[33,16,128]{2,1,0:T(8,128)}, u32[]{:S(2)}, u32[]{:S(2)}) collective-permute-start(f32[33,16,128]{2,1,0:T(8,128)} %get-tuple-element.23), channel_id=1, source_target_pairs={{0,6},{2,4},{4,2},{6,0},{1,7},{3,5},{5,3},{7,1},{8,14},{10,12},{12... | collective-permute-start | bytes 811016 | tf_op jit(solution)/shard_map/ppermute | solution.py:370
  8.6 4.0 %all-to-all-start = ((f32[32,8,128]{2,1,0:T(8,128)}), f32[32,8,128]{2,1,0:T(8,128)S(1)}, u32[]{:S(2)}, u32[]{:S(2)}) async-start(f32[32,8,128]{2,1,0:T(8,128)} %get-tuple-element.15), calls=%async_computation | async-start | bytes 262144 | tf_op jit(solution)/shard_map/all_to_all | solution.py:390
  12.6 1.8 %collective-permute-start.4 = (f32[33,16,128]{2,1,0:T(8,128)}, f32[33,16,128]{2,1,0:T(8,128)}, u32[]{:S(2)}, u32[]{:S(2)}) collective-permute-start(f32[33,16,128]{2,1,0:T(8,128)} %get-tuple-element.24), channel_id=1, source_target_pairs={{0,2},{2,0},{4,6},{6,4},{1,3},{3,1},{5,7},{7,5},{8,10},{10,8},{12,... | collective-permute-start | bytes 811016 | tf_op jit(solution)/shard_map/ppermute | solution.py:370
  14.4 1.5 %collective-permute-start.5 = (f32[33,16,128]{2,1,0:T(8,128)}, f32[33,16,128]{2,1,0:T(8,128)}, u32[]{:S(2)}, u32[]{:S(2)}) collective-permute-start(f32[33,16,128]{2,1,0:T(8,128)} %get-tuple-element.25), channel_id=1, source_target_pairs={{0,4},{2,6},{4,0},{6,2},{1,5},{3,7},{5,1},{7,3},{8,12},{10,14},{12... | collective-permute-start | bytes 811016 | tf_op jit(solution)/shard_map/ppermute | solution.py:370
  15.9 0.0 copy-done.2
  15.9 0.4 start_rows.1.start_ref
  16.3 4.6 %all-to-all-done.tiles_ref = f32[32,8,128]{2,1,0:T(8,128)S(1)} async-done(((f32[32,8,128]{2,1,0:T(8,128)}), f32[32,8,128]{2,1,0:T(8,128)S(1)}, u32[]{:S(2)}, u32[]{:S(2)}) %all-to-all-start) | async-done | bytes 131104 | tf_op jit(solution)/shard_map/all_to_all | solution.py:390
  20.9 0.0 copy-done
  20.9 3.3 %basis_late.1 = (f32[16,128]{1,0:T(8,128)S(1)}, f32[16,33]{1,0:T(8,128)}, f32[26,16,128]{2,1,0:T(8,128)S(1)}, f32[26,16,128]{2,1,0:T(8,128)S(1)}, f32[26,16,128]...) custom-call(f32[32,8,128]{2,1,0:T(8,128)S(1)} %all-to-all-done.tiles_ref, f32[16,128]{1,0:T(8,128)S(1)} %start_rows.1.start_ref, ...), custom_call_target="tpu_custom_call" | custom-call | bytes 105000000 | tf_op jit(solution)/shard_map/basis_late/pallas_call | solution.py:233
  24.2 0.9 %collective-permute-start = (f32[26,16,128]{2,1,0:T(8,128)S(1)}, f32[26,16,128]{2,1,0:T(8,128)S(1)}, u32[]{:S(2)}, u32[]{:S(2)}) collective-permute-start(f32[26,16,128]{2,1,0:T(8,128)S(1)} %get-tuple-element.17), channel_id=1, source_target_pairs={{0,6},{2,4},{4,2},{6,0},{1,7},{3,5},{5,3},{7,1},{8,14},{10,12},{12... | collective-permute-start | bytes 638984 | tf_op jit(solution)/shard_map/ppermute | solution.py:370
  25.1 1.3 %collective-permute-start.1 = (f32[26,16,128]{2,1,0:T(8,128)S(1)}, f32[26,16,128]{2,1,0:T(8,128)S(1)}, u32[]{:S(2)}, u32[]{:S(2)}) collective-permute-start(f32[26,16,128]{2,1,0:T(8,128)S(1)} %get-tuple-element.18), channel_id=1, source_target_pairs={{0,2},{2,0},{4,6},{6,4},{1,3},{3,1},{5,7},{7,5},{8,10},{10,8},{12,... | collective-permute-start | bytes 638984 | tf_op jit(solution)/shard_map/ppermute | solution.py:370
  26.4 0.0 collective-permute-done.3.refs_1_
  26.4 1.3 %collective-permute-start.2 = (f32[26,16,128]{2,1,0:T(8,128)S(1)}, f32[26,16,128]{2,1,0:T(8,128)S(1)}, u32[]{:S(2)}, u32[]{:S(2)}) collective-permute-start(f32[26,16,128]{2,1,0:T(8,128)S(1)} %get-tuple-element.19), channel_id=1, source_target_pairs={{0,4},{2,6},{4,0},{6,2},{1,5},{3,7},{5,1},{7,3},{8,12},{10,14},{12... | collective-permute-start | bytes 638984 | tf_op jit(solution)/shard_map/ppermute | solution.py:370
  27.8 0.0 collective-permute-done.4.refs_2_
  27.8 0.0 collective-permute-done.5.refs_3_
  27.8 0.0 copy-done.1
  27.8 1.8 %ready_rows.1 = (bf16[192,2048]{1,0:T(8,128)(2,1)S(1)}, bf16[192,2048]{1,0:T(8,128)(2,1)S(1)}) custom-call(f32[16,128]{1,0:T(8,128)S(1)} %get-tuple-element.20.rows_ref, f32[26,16,128]{2,1,0:T(8,128)S(1)} %get-tuple-element.21.late_ref, f32[33,16,128]{2,1,0:T(8,128)S(1)} %copy-done.1, f32[33,16,128]{2,1,0:T(8,128)} %collective-permute-done.3.refs_1_, ...), custom_call_target="tpu_custom_call" | custom-call | tf_op jit(solution)/shard_map/ready_rows/pallas_call | solution.py:283
  29.5 3.8 %collective-permute-done.refs_0_ = f32[26,16,128]{2,1,0:T(8,128)S(1)} collective-permute-done((f32[26,16,128]{2,1,0:T(8,128)S(1)}, f32[26,16,128]{2,1,0:T(8,128)S(1)}, u32[]{:S(2)}, u32[]{:S(2)}) %collective-permute-start) | collective-permute-done | bytes 213024 | tf_op jit(solution)/shard_map/ppermute | solution.py:370
  33.3 2.6 %collective-permute-done.1.refs_1_ = f32[26,16,128]{2,1,0:T(8,128)S(1)} collective-permute-done((f32[26,16,128]{2,1,0:T(8,128)S(1)}, f32[26,16,128]{2,1,0:T(8,128)S(1)}, u32[]{:S(2)}, u32[]{:S(2)}) %collective-permute-start.1) | collective-permute-done | bytes 213024 | tf_op jit(solution)/shard_map/ppermute | solution.py:370
  35.9 1.1 %collective-permute-done.2.refs_2_ = f32[26,16,128]{2,1,0:T(8,128)S(1)} collective-permute-done((f32[26,16,128]{2,1,0:T(8,128)S(1)}, f32[26,16,128]{2,1,0:T(8,128)S(1)}, u32[]{:S(2)}, u32[]{:S(2)}) %collective-permute-start.2) | collective-permute-done | bytes 213024 | tf_op jit(solution)/shard_map/ppermute | solution.py:370
  37.0 1.2 %line_tiles.1 = f32[32,8,128]{2,1,0:T(8,128)S(1)} custom-call(f32[26,16,128]{2,1,0:T(8,128)S(1)} %collective-permute-done.refs_0_, f32[26,16,128]{2,1,0:T(8,128)S(1)} %collective-permute-done.1.refs_1_, f32[26,16,128]{2,1,0:T(8,128)S(1)} %collective-permute-done.2.refs_2_, bf16[192,2048]{1,0:T(8,128)(2,1)S(1)} %get-tuple-element.26.refs_3_, ...), custom_call_target="tpu_custom_call" | custom-call | tf_op jit(solution)/shard_map/line_tiles/pallas_call | solution.py:336
  38.2 10.6 %all_to_all.10.tiles_ref = f32[32,8,128]{2,1,0:T(8,128)S(1)} all-to-all(f32[32,8,128]{2,1,0:T(8,128)S(1)} %line_tiles.1), channel_id=1, replica_groups=mesh['gx'=4,'gy'=4,'sa'=2] {'gx','gy','sa'}, dimensions={0} | all-to-all | bytes 262144 | tf_op jit(solution)/shard_map/all_to_all | solution.py:427
  48.9 0.7 %own_block.1 = f32[21,42]{1,0:T(8,128)} custom-call(f32[32,8,128]{2,1,0:T(8,128)S(1)} %all_to_all.10.tiles_ref), custom_call_target="tpu_custom_call" | custom-call | tf_op jit(solution)/shard_map/own_block/pallas_call | solution.py:191
  (1 shorter events, 0.0 us)
Async XLA Ops:
  0.6 20.3 %copy-start = (f32[33,4,42,128]{3,1,2,0:T(4,128)S(1)}, f32[33,4,42,128]{3,1,2,0:T(4,128)}, u32[]{:S(2)}) copy-start(f32[33,4,42,128]{3,1,2,0:T(4,128)} %param.2) | copy-start | bytes 8515588
  0.6 15.2 %copy-start.2 = (f32[33,16]{0,1:T(8,128)S(1)}, f32[33,16]{0,1:T(8,128)}, u32[]{:S(2)}) copy-start(f32[33,16]{0,1:T(8,128)} %param.3) | copy-start | bytes 6340
  4.6 23.1 %copy-start.1 = (f32[33,16,128]{2,1,0:T(8,128)S(1)}, f32[33,16,128]{2,1,0:T(8,128)}, u32[]{:S(2)}) copy-start(f32[33,16,128]{2,1,0:T(8,128)} %get-tuple-element.22.refs_0_) | copy-start | bytes 811012
  4.6 21.8 %collective-permute-start.3 = (f32[33,16,128]{2,1,0:T(8,128)}, f32[33,16,128]{2,1,0:T(8,128)}, u32[]{:S(2)}, u32[]{:S(2)}) collective-permute-start(f32[33,16,128]{2,1,0:T(8,128)} %get-tuple-element.23), channel_id=1, source_target_pairs={{0,6},{2,4},{4,2},{6,0},{1,7},{3,5},{5,3},{7,1},{8,14},{10,12},{12... | collective-permute-start | bytes 811016 | tf_op jit(solution)/shard_map/ppermute | solution.py:370
  8.6 12.3 %all-to-all-start = ((f32[32,8,128]{2,1,0:T(8,128)}), f32[32,8,128]{2,1,0:T(8,128)S(1)}, u32[]{:S(2)}, u32[]{:S(2)}) async-start(f32[32,8,128]{2,1,0:T(8,128)} %get-tuple-element.15), calls=%async_computation | async-start | bytes 262144 | tf_op jit(solution)/shard_map/all_to_all | solution.py:390
  12.6 15.2 %collective-permute-start.4 = (f32[33,16,128]{2,1,0:T(8,128)}, f32[33,16,128]{2,1,0:T(8,128)}, u32[]{:S(2)}, u32[]{:S(2)}) collective-permute-start(f32[33,16,128]{2,1,0:T(8,128)} %get-tuple-element.24), channel_id=1, source_target_pairs={{0,2},{2,0},{4,6},{6,4},{1,3},{3,1},{5,7},{7,5},{8,10},{10,8},{12,... | collective-permute-start | bytes 811016 | tf_op jit(solution)/shard_map/ppermute | solution.py:370
  14.4 13.4 %collective-permute-start.5 = (f32[33,16,128]{2,1,0:T(8,128)}, f32[33,16,128]{2,1,0:T(8,128)}, u32[]{:S(2)}, u32[]{:S(2)}) collective-permute-start(f32[33,16,128]{2,1,0:T(8,128)} %get-tuple-element.25), channel_id=1, source_target_pairs={{0,4},{2,6},{4,0},{6,2},{1,5},{3,7},{5,1},{7,3},{8,12},{10,14},{12... | collective-permute-start | bytes 811016 | tf_op jit(solution)/shard_map/ppermute | solution.py:370
  24.2 9.1 %collective-permute-start = (f32[26,16,128]{2,1,0:T(8,128)S(1)}, f32[26,16,128]{2,1,0:T(8,128)S(1)}, u32[]{:S(2)}, u32[]{:S(2)}) collective-permute-start(f32[26,16,128]{2,1,0:T(8,128)S(1)} %get-tuple-element.17), channel_id=1, source_target_pairs={{0,6},{2,4},{4,2},{6,0},{1,7},{3,5},{5,3},{7,1},{8,14},{10,12},{12... | collective-permute-start | bytes 638984 | tf_op jit(solution)/shard_map/ppermute | solution.py:370
  25.1 10.8 %collective-permute-start.1 = (f32[26,16,128]{2,1,0:T(8,128)S(1)}, f32[26,16,128]{2,1,0:T(8,128)S(1)}, u32[]{:S(2)}, u32[]{:S(2)}) collective-permute-start(f32[26,16,128]{2,1,0:T(8,128)S(1)} %get-tuple-element.18), channel_id=1, source_target_pairs={{0,2},{2,0},{4,6},{6,4},{1,3},{3,1},{5,7},{7,5},{8,10},{10,8},{12,... | collective-permute-start | bytes 638984 | tf_op jit(solution)/shard_map/ppermute | solution.py:370
  26.4 10.6 %collective-permute-start.2 = (f32[26,16,128]{2,1,0:T(8,128)S(1)}, f32[26,16,128]{2,1,0:T(8,128)S(1)}, u32[]{:S(2)}, u32[]{:S(2)}) collective-permute-start(f32[26,16,128]{2,1,0:T(8,128)S(1)} %get-tuple-element.19), channel_id=1, source_target_pairs={{0,4},{2,6},{4,0},{6,2},{1,5},{3,7},{5,1},{7,3},{8,12},{10,14},{12... | collective-permute-start | bytes 638984 | tf_op jit(solution)/shard_map/ppermute | solution.py:370

commit v4 on v3

--- a/solution.py
+++ b/solution.py
@@ -362,7 +362,7 @@
 def partners(size):
     if size & (size - 1):
         raise ValueError("axis size")
-    return sorted(range(size), key=lambda k: (k > 0, -k.bit_count(), k))
+    return sorted(range(size), key=lambda k: (k > 0, -k.bit_count(), -k))
 
 
 def exchanges(pieces, size):

time: 49.8 us -> 49.1 us (0.986)
  waiting for transfers between devices: 12.1 us -> 11.5 us
    ppermute x6, waiting for transfers between devices: 7.47 us -> 6.85 us  [exchanges(): lax.ppermute(piece, 'gy', [(a, a ^ k) for a in range(size)])]
  transfers between devices with their start and end apart: 7 -> 7, of which waited for: 4 -> 3; matrix products, arithmetic and copies ran while one was open for 0% -> 0% of each run, Pallas kernels for 11% -> 11%
where the time goes in v4:
time: 49.1 us; the launch traced here: 48.9 us
  starting transfers between devices  14.8 us (30%)
  waiting for transfers between devices  11.5 us (23%)
  Pallas kernels  11.4 us (23%)
  blocking collectives  10.5 us (21%)
  between operations  0.71 us (1%)
    ppermute x6, starting transfers between devices, exchanges(): lax.ppermute(piece, 'gy', [(a, a ^ k) for a in range(size)])  10.8 us
    all_to_all x1, blocking collectives, on_device(): blocks = lax.all_to_all(blocks, ALL, 0, 0, tiled=True)  10.5 us
    ppermute x6, waiting for transfers between devices, exchanges(): lax.ppermute(piece, 'gy', [(a, a ^ k) for a in range(size)])  6.85 us
    all_to_all x1, waiting for transfers between devices, on_device(): tiles = lax.all_to_all(tiles, ALL, 0, 0, tiled=True)  4.61 us
    pallas_call x1, Pallas kernels, gram_tiles(): pl.pallas_call(functools.partial(gram_kernel, cuts, cells_x), in_specs=[A...  3.97 us
    all_to_all x1, starting transfers between devices, on_device(): tiles = lax.all_to_all(tiles, ALL, 0, 0, tiled=True)  3.96 us
    pallas_call x1, Pallas kernels, basis_late(): pl.pallas_call(functools.partial(basis_late_kernel, scale, early * cells_...  3.27 us
    pallas_call x1, Pallas kernels, ready_rows(): pl.pallas_call(ready_kernel, in_specs=[VMEM] * (2 + len(pieces)), out_spe...  1.76 us
  transfers between devices with their start and end apart: 7, of which 3 were waited for; matrix products, arithmetic and copies ran while one was open for 0% of the time, Pallas kernels for 11%

profile of v4, /device:TPU:0, one launch (start us, length us, event | category | flops | bytes accessed | tf_op | source)
XLA Modules:
  0.0 48.9 jit_solution(17985521403476245325)
XLA Ops:
  0.6 0.0 copy-start
  0.6 0.0 copy-start.2
  0.6 4.0 %gram_tiles.1 = (f32[32,8,128]{2,1,0:T(8,128)}, f32[33,16,128]{2,1,0:T(8,128)}, f32[33,16,128]{2,1,0:T(8,128)}, f32[33,16,128]{2,1,0:T(8,128)}, f32[33,16,128]{2,1,0:T(8,128)}) custom-call(f32[33,168,128]{2,1,0:T(8,128)} %bitcast.6), custom_call_target="tpu_custom_call" | custom-call | tf_op jit(solution)/shard_map/gram_tiles/pallas_call | solution.py:109
  4.6 0.0 copy-start.1
  4.6 4.0 %collective-permute-start.3 = (f32[33,16,128]{2,1,0:T(8,128)}, f32[33,16,128]{2,1,0:T(8,128)}, u32[]{:S(2)}, u32[]{:S(2)}) collective-permute-start(f32[33,16,128]{2,1,0:T(8,128)} %get-tuple-element.23), channel_id=1, source_target_pairs={{0,6},{2,4},{4,2},{6,0},{1,7},{3,5},{5,3},{7,1},{8,14},{10,12},{12... | collective-permute-start | bytes 811016 | tf_op jit(solution)/shard_map/ppermute | solution.py:370
  8.6 4.0 %all-to-all-start = ((f32[32,8,128]{2,1,0:T(8,128)}), f32[32,8,128]{2,1,0:T(8,128)S(1)}, u32[]{:S(2)}, u32[]{:S(2)}) async-start(f32[32,8,128]{2,1,0:T(8,128)} %get-tuple-element.15), calls=%async_computation | async-start | bytes 262144 | tf_op jit(solution)/shard_map/all_to_all | solution.py:390
  12.6 1.8 %collective-permute-start.4 = (f32[33,16,128]{2,1,0:T(8,128)}, f32[33,16,128]{2,1,0:T(8,128)}, u32[]{:S(2)}, u32[]{:S(2)}) collective-permute-start(f32[33,16,128]{2,1,0:T(8,128)} %get-tuple-element.24), channel_id=1, source_target_pairs={{0,4},{2,6},{4,0},{6,2},{1,5},{3,7},{5,1},{7,3},{8,12},{10,14},{12... | collective-permute-start | bytes 811016 | tf_op jit(solution)/shard_map/ppermute | solution.py:370
  14.4 1.5 %collective-permute-start.5 = (f32[33,16,128]{2,1,0:T(8,128)}, f32[33,16,128]{2,1,0:T(8,128)}, u32[]{:S(2)}, u32[]{:S(2)}) collective-permute-start(f32[33,16,128]{2,1,0:T(8,128)} %get-tuple-element.25), channel_id=1, source_target_pairs={{0,2},{2,0},{4,6},{6,4},{1,3},{3,1},{5,7},{7,5},{8,10},{10,8},{12,... | collective-permute-start | bytes 811016 | tf_op jit(solution)/shard_map/ppermute | solution.py:370
  15.9 0.0 copy-done.2
  15.9 0.4 start_rows.1.start_ref
  16.3 4.6 %all-to-all-done.tiles_ref = f32[32,8,128]{2,1,0:T(8,128)S(1)} async-done(((f32[32,8,128]{2,1,0:T(8,128)}), f32[32,8,128]{2,1,0:T(8,128)S(1)}, u32[]{:S(2)}, u32[]{:S(2)}) %all-to-all-start) | async-done | bytes 131104 | tf_op jit(solution)/shard_map/all_to_all | solution.py:390
  20.9 0.0 copy-done
  20.9 3.3 %basis_late.1 = (f32[16,128]{1,0:T(8,128)S(1)}, f32[16,33]{1,0:T(8,128)}, f32[26,16,128]{2,1,0:T(8,128)S(1)}, f32[26,16,128]{2,1,0:T(8,128)S(1)}, f32[26,16,128]...) custom-call(f32[32,8,128]{2,1,0:T(8,128)S(1)} %all-to-all-done.tiles_ref, f32[16,128]{1,0:T(8,128)S(1)} %start_rows.1.start_ref, ...), custom_call_target="tpu_custom_call" | custom-call | bytes 105000000 | tf_op jit(solution)/shard_map/basis_late/pallas_call | solution.py:233
  24.2 0.9 %collective-permute-start = (f32[26,16,128]{2,1,0:T(8,128)S(1)}, f32[26,16,128]{2,1,0:T(8,128)S(1)}, u32[]{:S(2)}, u32[]{:S(2)}) collective-permute-start(f32[26,16,128]{2,1,0:T(8,128)S(1)} %get-tuple-element.17), channel_id=1, source_target_pairs={{0,6},{2,4},{4,2},{6,0},{1,7},{3,5},{5,3},{7,1},{8,14},{10,12},{12... | collective-permute-start | bytes 638984 | tf_op jit(solution)/shard_map/ppermute | solution.py:370
  25.1 1.0 %collective-permute-start.1 = (f32[26,16,128]{2,1,0:T(8,128)S(1)}, f32[26,16,128]{2,1,0:T(8,128)S(1)}, u32[]{:S(2)}, u32[]{:S(2)}) collective-permute-start(f32[26,16,128]{2,1,0:T(8,128)S(1)} %get-tuple-element.18), channel_id=1, source_target_pairs={{0,4},{2,6},{4,0},{6,2},{1,5},{3,7},{5,1},{7,3},{8,12},{10,14},{12... | collective-permute-start | bytes 638984 | tf_op jit(solution)/shard_map/ppermute | solution.py:370
  26.1 0.0 collective-permute-done.3.refs_1_
  26.1 1.7 %collective-permute-start.2 = (f32[26,16,128]{2,1,0:T(8,128)S(1)}, f32[26,16,128]{2,1,0:T(8,128)S(1)}, u32[]{:S(2)}, u32[]{:S(2)}) collective-permute-start(f32[26,16,128]{2,1,0:T(8,128)S(1)} %get-tuple-element.19), channel_id=1, source_target_pairs={{0,2},{2,0},{4,6},{6,4},{1,3},{3,1},{5,7},{7,5},{8,10},{10,8},{12,... | collective-permute-start | bytes 638984 | tf_op jit(solution)/shard_map/ppermute | solution.py:370
  27.7 0.0 collective-permute-done.4.refs_2_
  27.8 0.0 collective-permute-done.5.refs_3_
  27.8 0.0 copy-done.1
  27.8 1.8 %ready_rows.1 = (bf16[192,2048]{1,0:T(8,128)(2,1)S(1)}, bf16[192,2048]{1,0:T(8,128)(2,1)S(1)}) custom-call(f32[16,128]{1,0:T(8,128)S(1)} %get-tuple-element.20.rows_ref, f32[26,16,128]{2,1,0:T(8,128)S(1)} %get-tuple-element.21.late_ref, f32[33,16,128]{2,1,0:T(8,128)S(1)} %copy-done.1, f32[33,16,128]{2,1,0:T(8,128)} %collective-permute-done.3.refs_1_, ...), custom_call_target="tpu_custom_call" | custom-call | tf_op jit(solution)/shard_map/ready_rows/pallas_call | solution.py:283
  29.5 3.8 %collective-permute-done.refs_0_ = f32[26,16,128]{2,1,0:T(8,128)S(1)} collective-permute-done((f32[26,16,128]{2,1,0:T(8,128)S(1)}, f32[26,16,128]{2,1,0:T(8,128)S(1)}, u32[]{:S(2)}, u32[]{:S(2)}) %collective-permute-start) | collective-permute-done | bytes 213024 | tf_op jit(solution)/shard_map/ppermute | solution.py:370
  33.3 3.1 %collective-permute-done.1.refs_1_ = f32[26,16,128]{2,1,0:T(8,128)S(1)} collective-permute-done((f32[26,16,128]{2,1,0:T(8,128)S(1)}, f32[26,16,128]{2,1,0:T(8,128)S(1)}, u32[]{:S(2)}, u32[]{:S(2)}) %collective-permute-start.1) | collective-permute-done | bytes 213024 | tf_op jit(solution)/shard_map/ppermute | solution.py:370
  36.4 0.0 collective-permute-done.2.refs_2_
  36.4 1.2 %line_tiles.1 = f32[32,8,128]{2,1,0:T(8,128)S(1)} custom-call(f32[26,16,128]{2,1,0:T(8,128)S(1)} %collective-permute-done.refs_0_, f32[26,16,128]{2,1,0:T(8,128)S(1)} %collective-permute-done.1.refs_1_, f32[26,16,128]{2,1,0:T(8,128)S(1)} %collective-permute-done.2.refs_2_, bf16[192,2048]{1,0:T(8,128)(2,1)S(1)} %get-tuple-element.26.refs_3_, ...), custom_call_target="tpu_custom_call" | custom-call | tf_op jit(solution)/shard_map/line_tiles/pallas_call | solution.py:336
  37.6 10.5 %all_to_all.10.tiles_ref = f32[32,8,128]{2,1,0:T(8,128)S(1)} all-to-all(f32[32,8,128]{2,1,0:T(8,128)S(1)} %line_tiles.1), channel_id=1, replica_groups=mesh['gx'=4,'gy'=4,'sa'=2] {'gx','gy','sa'}, dimensions={0} | all-to-all | bytes 262144 | tf_op jit(solution)/shard_map/all_to_all | solution.py:427
  48.2 0.7 %own_block.1 = f32[21,42]{1,0:T(8,128)} custom-call(f32[32,8,128]{2,1,0:T(8,128)S(1)} %all_to_all.10.tiles_ref), custom_call_target="tpu_custom_call" | custom-call | tf_op jit(solution)/shard_map/own_block/pallas_call | solution.py:191
  (1 shorter events, 0.0 us)
Async XLA Ops:
  0.6 20.3 %copy-start = (f32[33,4,42,128]{3,1,2,0:T(4,128)S(1)}, f32[33,4,42,128]{3,1,2,0:T(4,128)}, u32[]{:S(2)}) copy-start(f32[33,4,42,128]{3,1,2,0:T(4,128)} %param.2) | copy-start | bytes 8515588
  0.6 15.2 %copy-start.2 = (f32[33,16]{0,1:T(8,128)S(1)}, f32[33,16]{0,1:T(8,128)}, u32[]{:S(2)}) copy-start(f32[33,16]{0,1:T(8,128)} %param.3) | copy-start | bytes 6340
  4.6 23.1 %copy-start.1 = (f32[33,16,128]{2,1,0:T(8,128)S(1)}, f32[33,16,128]{2,1,0:T(8,128)}, u32[]{:S(2)}) copy-start(f32[33,16,128]{2,1,0:T(8,128)} %get-tuple-element.22.refs_0_) | copy-start | bytes 811012
  4.6 21.4 %collective-permute-start.3 = (f32[33,16,128]{2,1,0:T(8,128)}, f32[33,16,128]{2,1,0:T(8,128)}, u32[]{:S(2)}, u32[]{:S(2)}) collective-permute-start(f32[33,16,128]{2,1,0:T(8,128)} %get-tuple-element.23), channel_id=1, source_target_pairs={{0,6},{2,4},{4,2},{6,0},{1,7},{3,5},{5,3},{7,1},{8,14},{10,12},{12... | collective-permute-start | bytes 811016 | tf_op jit(solution)/shard_map/ppermute | solution.py:370
  8.6 12.3 %all-to-all-start = ((f32[32,8,128]{2,1,0:T(8,128)}), f32[32,8,128]{2,1,0:T(8,128)S(1)}, u32[]{:S(2)}, u32[]{:S(2)}) async-start(f32[32,8,128]{2,1,0:T(8,128)} %get-tuple-element.15), calls=%async_computation | async-start | bytes 262144 | tf_op jit(solution)/shard_map/all_to_all | solution.py:390
  12.6 15.2 %collective-permute-start.4 = (f32[33,16,128]{2,1,0:T(8,128)}, f32[33,16,128]{2,1,0:T(8,128)}, u32[]{:S(2)}, u32[]{:S(2)}) collective-permute-start(f32[33,16,128]{2,1,0:T(8,128)} %get-tuple-element.24), channel_id=1, source_target_pairs={{0,4},{2,6},{4,0},{6,2},{1,5},{3,7},{5,1},{7,3},{8,12},{10,14},{12... | collective-permute-start | bytes 811016 | tf_op jit(solution)/shard_map/ppermute | solution.py:370
  14.4 13.3 %collective-permute-start.5 = (f32[33,16,128]{2,1,0:T(8,128)}, f32[33,16,128]{2,1,0:T(8,128)}, u32[]{:S(2)}, u32[]{:S(2)}) collective-permute-start(f32[33,16,128]{2,1,0:T(8,128)} %get-tuple-element.25), channel_id=1, source_target_pairs={{0,2},{2,0},{4,6},{6,4},{1,3},{3,1},{5,7},{7,5},{8,10},{10,8},{12,... | collective-permute-start | bytes 811016 | tf_op jit(solution)/shard_map/ppermute | solution.py:370
  24.2 9.1 %collective-permute-start = (f32[26,16,128]{2,1,0:T(8,128)S(1)}, f32[26,16,128]{2,1,0:T(8,128)S(1)}, u32[]{:S(2)}, u32[]{:S(2)}) collective-permute-start(f32[26,16,128]{2,1,0:T(8,128)S(1)} %get-tuple-element.17), channel_id=1, source_target_pairs={{0,6},{2,4},{4,2},{6,0},{1,7},{3,5},{5,3},{7,1},{8,14},{10,12},{12... | collective-permute-start | bytes 638984 | tf_op jit(solution)/shard_map/ppermute | solution.py:370
  25.1 11.3 %collective-permute-start.1 = (f32[26,16,128]{2,1,0:T(8,128)S(1)}, f32[26,16,128]{2,1,0:T(8,128)S(1)}, u32[]{:S(2)}, u32[]{:S(2)}) collective-permute-start(f32[26,16,128]{2,1,0:T(8,128)S(1)} %get-tuple-element.18), channel_id=1, source_target_pairs={{0,4},{2,6},{4,0},{6,2},{1,5},{3,7},{5,1},{7,3},{8,12},{10,14},{12... | collective-permute-start | bytes 638984 | tf_op jit(solution)/shard_map/ppermute | solution.py:370
  26.1 10.3 %collective-permute-start.2 = (f32[26,16,128]{2,1,0:T(8,128)S(1)}, f32[26,16,128]{2,1,0:T(8,128)S(1)}, u32[]{:S(2)}, u32[]{:S(2)}) collective-permute-start(f32[26,16,128]{2,1,0:T(8,128)S(1)} %get-tuple-element.19), channel_id=1, source_target_pairs={{0,2},{2,0},{4,6},{6,4},{1,3},{3,1},{5,7},{7,5},{8,10},{10,8},{12,... | collective-permute-start | bytes 638984 | tf_op jit(solution)/shard_map/ppermute | solution.py:370

commit v5 on v4

--- a/solution.py
+++ b/solution.py
@@ -80,7 +80,7 @@
     for i, (copy, span) in enumerate(zip(copies, spans, strict=True)):
         copy.wait()
         for k, send in enumerate(sends if i == 0 else ()):
-            early[k] = buffer[:, pl.ds(partner(partners(len(sends))[k]), early.shape[2], stride=cells_x), :]
+            early[k] = buffer[:, pl.ds(partner(partners(len(sends) + 1)[k + 1]), early.shape[2], stride=cells_x), :]
             send.start()
         both = stacked(buffer[:, span, :], pitch)
         total[: 2 * pitch, : 2 * pitch] += dot32(both, both, BY_LAST)
@@ -204,17 +204,14 @@
 
 def basis_late_kernel(scale, top, cells_x, tiles_ref, start_ref, field_ref, *refs):
     rows_ref, basis_ref = refs[:2]
-    late_refs, (buffer, core_ref, sem) = refs[2:-3], refs[-3:]
+    late_refs, core_ref = refs[2:-1], refs[-1]
     species, _, cells = field_ref.shape
     pitch = up(species, HALF_ROWS)
-    copy = pltpu.make_async_copy(field_ref.at[:, top:, :], buffer, sem)
-    copy.start()
     gram = unpacked(jnp.sum(tiles_ref[...], axis=0) * scale, species)
     rows = start_ref[...]
     for _ in range(ITERS - 1):
         rows = turn(rows, gram)
-    copy.wait()
-    stack = stacked(buffer[...], pitch)
+    stack = stacked(field_ref[:, top:, :], pitch)
     rows = turn(rows, gram)
     rows_ref[...] = rows
     basis_ref[...] = rows[:, :species]
@@ -232,7 +229,7 @@
     late = lines - early
     return pl.pallas_call(
         functools.partial(basis_late_kernel, scale, early * cells_x, cells_x),
-        in_specs=[VMEM, VMEM, ANY],
+        in_specs=[VMEM, VMEM, VMEM],
         out_specs=[VMEM] * (2 + count),
         out_shape=[
             jax.ShapeDtypeStruct((ranks, LANES), jnp.float32),
@@ -240,9 +237,7 @@
         ]
         + [jax.ShapeDtypeStruct((late, ranks, cells), jnp.float32)] * count,
         scratch_shapes=[
-            pltpu.VMEM((species, late * cells_x, cells), jnp.float32),
             pltpu.VMEM((late * cells_x, ranks, cells), jnp.float32),
-            pltpu.SemaphoreType.DMA,
         ],
         compiler_params=MIDDLE,
         cost_estimate=lasting(30),
@@ -261,14 +256,19 @@
     low_ref[pl.ds(at, block.shape[0]), :] = low
 
 
-def ready_kernel(rows_ref, late_ref, *refs):
+def ready_kernel(cells_x, rows_ref, late_ref, field_ref, *refs):
     pieces, (high_ref, low_ref, part_ref) = refs[:-3], refs[-3:]
-    pitch = high_ref.shape[0] // len(pieces)
+    size = len(pieces) + 1
+    pitch = high_ref.shape[0] // size
     species, early, cells = pieces[0].shape
     wide = up(species, HALF_ROWS)
     left = doubled(rows_ref[...], wide)
-    for k, piece in zip(partners(len(pieces)), pieces, strict=True):
-        core = projected(left, stacked(piece[...], wide))
+    for i, k in enumerate(partners(size)):
+        if k == 0:
+            piece = field_ref[:, pl.ds(partner(0), early, stride=cells_x), :]
+        else:
+            piece = pieces[i - 1][...]
+        core = projected(left, stacked(piece, wide))
         for y in range(early):
             part_ref[y] = core[:, y * cells : (y + 1) * cells]
         place(part_ref[...], pl.multiple_of(partner(k) * pitch, HALF_ROWS), high_ref, low_ref)
@@ -276,19 +276,19 @@
     place(late_ref[...], at, high_ref, low_ref)
 
 
-def ready_rows(rows, own, pieces, lines):
-    species, early, cells = pieces[0].shape
+def ready_rows(rows, own, field, pieces, lines):
+    _, early, cells = pieces[0].shape
     ranks = rows.shape[0]
-    shape = (len(pieces) * up(lines, HALF_ROWS), ranks * cells)
+    shape = ((len(pieces) + 1) * up(lines, HALF_ROWS), ranks * cells)
     return pl.pallas_call(
-        ready_kernel,
-        in_specs=[VMEM] * (2 + len(pieces)),
+        functools.partial(ready_kernel, field.shape[1]),
+        in_specs=[VMEM] * (3 + len(pieces)),
         out_specs=[VMEM, VMEM],
         out_shape=[jax.ShapeDtypeStruct(shape, jnp.bfloat16)] * 2,
         scratch_shapes=[pltpu.VMEM((early, ranks, cells), jnp.float32)],
         compiler_params=PARAMS,
         name="ready_rows",
-    )(rows, own, *pieces)
+    )(rows, own, by_rows(field), *pieces)
 
 
 def packing(lines, columns):
@@ -366,9 +366,9 @@
 
 
 def exchanges(pieces, size):
-    return pieces[:1] + [
+    return [
         lax.ppermute(piece, "gy", [(a, a ^ k) for a in range(size)])
-        for k, piece in zip(partners(size)[1:], pieces[1:], strict=True)
+        for k, piece in zip(partners(size)[1:], pieces, strict=True)
     ]
 
 
@@ -386,7 +386,7 @@
     by_x = parts_x == cells_x and parts_z == 1 and early > 0
     early = early if by_x else 0
 
-    tiles, *outgoing = gram_tiles(field, devices, early, n_gy if by_x else 0)
+    tiles, *outgoing = gram_tiles(field, devices, early, n_gy - 1 if by_x else 0)
     tiles = lax.all_to_all(tiles, ALL, 0, 0, tiled=True)
     first = whole_call(
         start_kernel,
@@ -398,8 +398,8 @@
     if by_x:
         received = exchanges(outgoing, n_gy)
         rows, basis, own, *pieces = basis_late(scale, early, n_gy, tiles, first, field)
-        own, *pieces = exchanges([own, *pieces], n_gy)
-        ready = ready_rows(rows, own, received, lines)
+        pieces = exchanges(pieces, n_gy)
+        ready = ready_rows(rows, own, field, received, lines)
     else:
         rows, basis = whole_call(
             functools.partial(basis_kernel, species, scale),
@@ -422,7 +422,7 @@
                 (lines, ranks, wide_x, wide_z),
             )
             pieces.append(cut.reshape(lines, -1, LANES))
-        pieces = exchanges(pieces, n_gy)
+        pieces = pieces[:1] + exchanges(pieces[1:], n_gy)
     blocks = line_tiles(pieces, ready, axes, lines, early)
     blocks = lax.all_to_all(blocks, ALL, 0, 0, tiled=True)
     block = whole_call(

time: 49.1 us -> 48.9 us (level)
  no operation moved by 1% of the time
where the time goes in v5:
time: 48.9 us; the launch traced here: 48.7 us
  starting transfers between devices  14.8 us (30%)
  waiting for transfers between devices  11.5 us (24%)
  Pallas kernels  11.1 us (23%)
  blocking collectives  10.5 us (21%)
  between operations  0.7 us (1%)
    ppermute x6, starting transfers between devices, exchanges(): lax.ppermute(piece, 'gy', [(a, a ^ k) for a in range(size)])  10.8 us
    all_to_all x1, blocking collectives, on_device(): blocks = lax.all_to_all(blocks, ALL, 0, 0, tiled=True)  10.5 us
    ppermute x6, waiting for transfers between devices, exchanges(): lax.ppermute(piece, 'gy', [(a, a ^ k) for a in range(size)])  6.94 us
    all_to_all x1, waiting for transfers between devices, on_device(): tiles = lax.all_to_all(tiles, ALL, 0, 0, tiled=True)  4.61 us
    all_to_all x1, starting transfers between devices, on_device(): tiles = lax.all_to_all(tiles, ALL, 0, 0, tiled=True)  3.97 us
    pallas_call x1, Pallas kernels, gram_tiles(): pl.pallas_call(functools.partial(gram_kernel, cuts, cells_x), in_specs=[A...  3.93 us
    pallas_call x1, Pallas kernels, basis_late(): pl.pallas_call(functools.partial(basis_late_kernel, scale, early * cells_...  3.15 us
    pallas_call x1, Pallas kernels, ready_rows(): pl.pallas_call(functools.partial(ready_kernel, field.shape[1]), in_specs=...  1.68 us
  transfers between devices with their start and end apart: 7, of which 3 were waited for; matrix products, arithmetic and copies ran while one was open for 0% of the time, Pallas kernels for 11%

profile of v5, /device:TPU:0, one launch (start us, length us, event | category | flops | bytes accessed | tf_op | source)
XLA Modules:
  0.0 48.7 jit_solution(7740986770283202533)
XLA Ops:
  0.6 0.0 copy-start
  0.6 0.0 copy-start.1
  0.6 3.9 %gram_tiles.1 = (f32[32,8,128]{2,1,0:T(8,128)}, f32[33,16,128]{2,1,0:T(8,128)}, f32[33,16,128]{2,1,0:T(8,128)}, f32[33,16,128]{2,1,0:T(8,128)}) custom-call(f32[33,168,128]{2,1,0:T(8,128)} %bitcast.6), custom_call_target="tpu_custom_call" | custom-call | tf_op jit(solution)/shard_map/gram_tiles/pallas_call | solution.py:109
  4.6 4.0 %collective-permute-start.3 = (f32[33,16,128]{2,1,0:T(8,128)}, f32[33,16,128]{2,1,0:T(8,128)S(1)}, u32[]{:S(2)}, u32[]{:S(2)}) collective-permute-start(f32[33,16,128]{2,1,0:T(8,128)} %get-tuple-element.21), channel_id=1, source_target_pairs={{0,6},{2,4},{4,2},{6,0},{1,7},{3,5},{5,3},{7,1},{8,14},{10,12},{12... | collective-permute-start | bytes 811016 | tf_op jit(solution)/shard_map/ppermute | solution.py:370
  8.5 4.0 %all-to-all-start = ((f32[32,8,128]{2,1,0:T(8,128)}), f32[32,8,128]{2,1,0:T(8,128)S(1)}, u32[]{:S(2)}, u32[]{:S(2)}) async-start(f32[32,8,128]{2,1,0:T(8,128)} %get-tuple-element.14), calls=%async_computation | async-start | bytes 262144 | tf_op jit(solution)/shard_map/all_to_all | solution.py:390
  12.5 1.8 %collective-permute-start.4 = (f32[33,16,128]{2,1,0:T(8,128)}, f32[33,16,128]{2,1,0:T(8,128)}, u32[]{:S(2)}, u32[]{:S(2)}) collective-permute-start(f32[33,16,128]{2,1,0:T(8,128)} %get-tuple-element.22), channel_id=1, source_target_pairs={{0,4},{2,6},{4,0},{6,2},{1,5},{3,7},{5,1},{7,3},{8,12},{10,14},{12... | collective-permute-start | bytes 811016 | tf_op jit(solution)/shard_map/ppermute | solution.py:370
  14.4 1.5 %collective-permute-start.5 = (f32[33,16,128]{2,1,0:T(8,128)}, f32[33,16,128]{2,1,0:T(8,128)}, u32[]{:S(2)}, u32[]{:S(2)}) collective-permute-start(f32[33,16,128]{2,1,0:T(8,128)} %get-tuple-element.23), channel_id=1, source_target_pairs={{0,2},{2,0},{4,6},{6,4},{1,3},{3,1},{5,7},{7,5},{8,10},{10,8},{12,... | collective-permute-start | bytes 811016 | tf_op jit(solution)/shard_map/ppermute | solution.py:370
  15.8 0.0 copy-done.1
  15.8 0.4 start_rows.1.start_ref
  16.2 4.6 %all-to-all-done.tiles_ref = f32[32,8,128]{2,1,0:T(8,128)S(1)} async-done(((f32[32,8,128]{2,1,0:T(8,128)}), f32[32,8,128]{2,1,0:T(8,128)S(1)}, u32[]{:S(2)}, u32[]{:S(2)}) %all-to-all-start) | async-done | bytes 131104 | tf_op jit(solution)/shard_map/all_to_all | solution.py:390
  20.9 0.0 copy-done
  20.9 3.2 %basis_late.1 = (f32[16,128]{1,0:T(8,128)S(1)}, f32[16,33]{1,0:T(8,128)}, f32[26,16,128]{2,1,0:T(8,128)S(1)}, f32[26,16,128]{2,1,0:T(8,128)S(1)}, f32[26,16,128]...) custom-call(f32[32,8,128]{2,1,0:T(8,128)S(1)} %all-to-all-done.tiles_ref, f32[16,128]{1,0:T(8,128)S(1)} %start_rows.1.start_ref, ...), custom_call_target="tpu_custom_call" | custom-call | bytes 105000000 | tf_op jit(solution)/shard_map/basis_late/pallas_call | solution.py:230
  24.0 0.9 %collective-permute-start = (f32[26,16,128]{2,1,0:T(8,128)S(1)}, f32[26,16,128]{2,1,0:T(8,128)S(1)}, u32[]{:S(2)}, u32[]{:S(2)}) collective-permute-start(f32[26,16,128]{2,1,0:T(8,128)S(1)} %get-tuple-element.16), channel_id=1, source_target_pairs={{0,6},{2,4},{4,2},{6,0},{1,7},{3,5},{5,3},{7,1},{8,14},{10,12},{12... | collective-permute-start | bytes 638984 | tf_op jit(solution)/shard_map/ppermute | solution.py:370
  24.9 1.0 %collective-permute-start.1 = (f32[26,16,128]{2,1,0:T(8,128)S(1)}, f32[26,16,128]{2,1,0:T(8,128)S(1)}, u32[]{:S(2)}, u32[]{:S(2)}) collective-permute-start(f32[26,16,128]{2,1,0:T(8,128)S(1)} %get-tuple-element.17), channel_id=1, source_target_pairs={{0,4},{2,6},{4,0},{6,2},{1,5},{3,7},{5,1},{7,3},{8,12},{10,14},{12... | collective-permute-start | bytes 638984 | tf_op jit(solution)/shard_map/ppermute | solution.py:370
  25.9 0.0 collective-permute-done.3.refs_0_
  25.9 1.7 %collective-permute-start.2 = (f32[26,16,128]{2,1,0:T(8,128)S(1)}, f32[26,16,128]{2,1,0:T(8,128)S(1)}, u32[]{:S(2)}, u32[]{:S(2)}) collective-permute-start(f32[26,16,128]{2,1,0:T(8,128)S(1)} %get-tuple-element.18), channel_id=1, source_target_pairs={{0,2},{2,0},{4,6},{6,4},{1,3},{3,1},{5,7},{7,5},{8,10},{10,8},{12,... | collective-permute-start | bytes 638984 | tf_op jit(solution)/shard_map/ppermute | solution.py:370
  27.6 0.0 collective-permute-done.4.refs_1_
  27.6 0.0 collective-permute-done.5.refs_2_
  27.6 1.7 %ready_rows.1 = (bf16[192,2048]{1,0:T(8,128)(2,1)S(1)}, bf16[192,2048]{1,0:T(8,128)(2,1)S(1)}) custom-call(f32[16,128]{1,0:T(8,128)S(1)} %get-tuple-element.19.rows_ref, f32[26,16,128]{2,1,0:T(8,128)S(1)} %get-tuple-element.20.late_ref, f32[33,168,128]{2,1,0:T(8,128)S(1)} %bitcast.8, f32[33,16,128]{2,1,0:T(8,128)S(1)} %collective-permute-done.3.refs_0_, ...), custom_call_target="tpu_custom_call" | custom-call | tf_op jit(solution)/shard_map/ready_rows/pallas_call | solution.py:283
  29.3 3.9 %collective-permute-done.refs_0_ = f32[26,16,128]{2,1,0:T(8,128)S(1)} collective-permute-done((f32[26,16,128]{2,1,0:T(8,128)S(1)}, f32[26,16,128]{2,1,0:T(8,128)S(1)}, u32[]{:S(2)}, u32[]{:S(2)}) %collective-permute-start) | collective-permute-done | bytes 213024 | tf_op jit(solution)/shard_map/ppermute | solution.py:370
  33.1 3.1 %collective-permute-done.1.refs_1_ = f32[26,16,128]{2,1,0:T(8,128)S(1)} collective-permute-done((f32[26,16,128]{2,1,0:T(8,128)S(1)}, f32[26,16,128]{2,1,0:T(8,128)S(1)}, u32[]{:S(2)}, u32[]{:S(2)}) %collective-permute-start.1) | collective-permute-done | bytes 213024 | tf_op jit(solution)/shard_map/ppermute | solution.py:370
  36.2 0.0 collective-permute-done.2.refs_2_
  36.2 1.2 %line_tiles.1 = f32[32,8,128]{2,1,0:T(8,128)S(1)} custom-call(f32[26,16,128]{2,1,0:T(8,128)S(1)} %collective-permute-done.refs_0_, f32[26,16,128]{2,1,0:T(8,128)S(1)} %collective-permute-done.1.refs_1_, f32[26,16,128]{2,1,0:T(8,128)S(1)} %collective-permute-done.2.refs_2_, bf16[192,2048]{1,0:T(8,128)(2,1)S(1)} %get-tuple-element.24.refs_3_, ...), custom_call_target="tpu_custom_call" | custom-call | tf_op jit(solution)/shard_map/line_tiles/pallas_call | solution.py:336
  37.4 10.5 %all_to_all.10.tiles_ref = f32[32,8,128]{2,1,0:T(8,128)S(1)} all-to-all(f32[32,8,128]{2,1,0:T(8,128)S(1)} %line_tiles.1), channel_id=1, replica_groups=mesh['gx'=4,'gy'=4,'sa'=2] {'gx','gy','sa'}, dimensions={0} | all-to-all | bytes 262144 | tf_op jit(solution)/shard_map/all_to_all | solution.py:427
  48.0 0.7 %own_block.1 = f32[21,42]{1,0:T(8,128)} custom-call(f32[32,8,128]{2,1,0:T(8,128)S(1)} %all_to_all.10.tiles_ref), custom_call_target="tpu_custom_call" | custom-call | tf_op jit(solution)/shard_map/own_block/pallas_call | solution.py:191
  (1 shorter events, 0.0 us)
Async XLA Ops:
  0.6 20.2 %copy-start = (f32[33,4,42,128]{3,1,2,0:T(4,128)S(1)}, f32[33,4,42,128]{3,1,2,0:T(4,128)}, u32[]{:S(2)}) copy-start(f32[33,4,42,128]{3,1,2,0:T(4,128)} %param.2) | copy-start | bytes 8515588
  0.6 15.2 %copy-start.1 = (f32[33,16]{0,1:T(8,128)S(1)}, f32[33,16]{0,1:T(8,128)}, u32[]{:S(2)}) copy-start(f32[33,16]{0,1:T(8,128)} %param.3) | copy-start | bytes 6340
  4.6 21.3 %collective-permute-start.3 = (f32[33,16,128]{2,1,0:T(8,128)}, f32[33,16,128]{2,1,0:T(8,128)S(1)}, u32[]{:S(2)}, u32[]{:S(2)}) collective-permute-start(f32[33,16,128]{2,1,0:T(8,128)} %get-tuple-element.21), channel_id=1, source_target_pairs={{0,6},{2,4},{4,2},{6,0},{1,7},{3,5},{5,3},{7,1},{8,14},{10,12},{12... | collective-permute-start | bytes 811016 | tf_op jit(solution)/shard_map/ppermute | solution.py:370
  8.5 12.3 %all-to-all-start = ((f32[32,8,128]{2,1,0:T(8,128)}), f32[32,8,128]{2,1,0:T(8,128)S(1)}, u32[]{:S(2)}, u32[]{:S(2)}) async-start(f32[32,8,128]{2,1,0:T(8,128)} %get-tuple-element.14), calls=%async_computation | async-start | bytes 262144 | tf_op jit(solution)/shard_map/all_to_all | solution.py:390
  12.5 15.1 %collective-permute-start.4 = (f32[33,16,128]{2,1,0:T(8,128)}, f32[33,16,128]{2,1,0:T(8,128)}, u32[]{:S(2)}, u32[]{:S(2)}) collective-permute-start(f32[33,16,128]{2,1,0:T(8,128)} %get-tuple-element.22), channel_id=1, source_target_pairs={{0,4},{2,6},{4,0},{6,2},{1,5},{3,7},{5,1},{7,3},{8,12},{10,14},{12... | collective-permute-start | bytes 811016 | tf_op jit(solution)/shard_map/ppermute | solution.py:370
  14.4 13.2 %collective-permute-start.5 = (f32[33,16,128]{2,1,0:T(8,128)}, f32[33,16,128]{2,1,0:T(8,128)}, u32[]{:S(2)}, u32[]{:S(2)}) collective-permute-start(f32[33,16,128]{2,1,0:T(8,128)} %get-tuple-element.23), channel_id=1, source_target_pairs={{0,2},{2,0},{4,6},{6,4},{1,3},{3,1},{5,7},{7,5},{8,10},{10,8},{12,... | collective-permute-start | bytes 811016 | tf_op jit(solution)/shard_map/ppermute | solution.py:370
  24.0 9.1 %collective-permute-start = (f32[26,16,128]{2,1,0:T(8,128)S(1)}, f32[26,16,128]{2,1,0:T(8,128)S(1)}, u32[]{:S(2)}, u32[]{:S(2)}) collective-permute-start(f32[26,16,128]{2,1,0:T(8,128)S(1)} %get-tuple-element.16), channel_id=1, source_target_pairs={{0,6},{2,4},{4,2},{6,0},{1,7},{3,5},{5,3},{7,1},{8,14},{10,12},{12... | collective-permute-start | bytes 638984 | tf_op jit(solution)/shard_map/ppermute | solution.py:370
  24.9 11.3 %collective-permute-start.1 = (f32[26,16,128]{2,1,0:T(8,128)S(1)}, f32[26,16,128]{2,1,0:T(8,128)S(1)}, u32[]{:S(2)}, u32[]{:S(2)}) collective-permute-start(f32[26,16,128]{2,1,0:T(8,128)S(1)} %get-tuple-element.17), channel_id=1, source_target_pairs={{0,4},{2,6},{4,0},{6,2},{1,5},{3,7},{5,1},{7,3},{8,12},{10,14},{12... | collective-permute-start | bytes 638984 | tf_op jit(solution)/shard_map/ppermute | solution.py:370
  25.9 10.3 %collective-permute-start.2 = (f32[26,16,128]{2,1,0:T(8,128)S(1)}, f32[26,16,128]{2,1,0:T(8,128)S(1)}, u32[]{:S(2)}, u32[]{:S(2)}) collective-permute-start(f32[26,16,128]{2,1,0:T(8,128)S(1)} %get-tuple-element.18), channel_id=1, source_target_pairs={{0,2},{2,0},{4,6},{6,4},{1,3},{3,1},{5,7},{7,5},{8,10},{10,8},{12,... | collective-permute-start | bytes 638984 | tf_op jit(solution)/shard_map/ppermute | solution.py:370
